TPU v7x, 256 devices: a whole 4x4x8 slice. The times are simulated.
256 devices in a mesh: lon: 64 (over x_lo, y, z), lat: 4 (over x_hi, core).
Axes of the slice: x: 4 (x_hi: 2, x_lo: 2; x = x_hi * 2 + x_lo), y: 4, z: 8, core: 2. Of those that a mesh axis runs over, the one named last changes fastest.
Arguments:
- air_state: bfloat16 [8, 48, 768, 192], P(None, 'lat', 'lon'), may hold values from -6 to 6
- cotangent: bfloat16 [8, 48, 768, 192], P(None, 'lat', 'lon'), may hold values from -6 to 6
- norm_gain: float32 [192], replicated, may hold values from 0.1 to 1.9
- norm_shift: float32 [192], replicated, may hold values from -3 to 3
- qkv_weight: bfloat16 [192, 576], replicated, may hold values from -0.4375 to 0.4375
- proj_weight: bfloat16 [192, 192], replicated, may hold values from -0.4375 to 0.4375
- earth_bias: float32 [8, 4, 6, 3312], P('lat'), may hold values from -4.5 to 250
Outputs:
- air_out: bfloat16 [8, 48, 768, 192], P(None, 'lat', 'lon')
- state_grad: bfloat16 [8, 48, 768, 192], P(None, 'lat', 'lon')
- qkv_grad: float32 [192, 576], replicated
- proj_grad: float32 [192, 192], replicated
- gain_grad: float32 [192], replicated
- shift_grad: float32 [192], replicated
- bias_grad: bfloat16 [8, 4, 6, 3312], P('lat')
All inputs are finite; a program needn't handle non-finite values.
Results may differ from a plain program's by a relative error of at most 0.01.
Values may be sent and summed in bfloat16 or wider, within the bound.
No kernel may reach another device: no remote copies, remote signals or barrier semaphores. Data moves between devices by JAX's collectives and lax.ppermute only.
A program may use at most 128 MiB of HBM per device.

v0:
```python
import functools
import math

import jax
import jax.numpy as jnp
import numpy as np
from jax import lax
from jax.experimental import pallas as pl
from jax.experimental.pallas import tpu as pltpu
from jax.sharding import Mesh, PartitionSpec as P

HEADS=6; WZ=2; WLAT=6; WLON=12; WTOK=144; POSITIONS=3312
C=192; HD=32
EPSILON=1e-5
MASKED=-1e30
QP=896
GL=72
F32=jnp.float32; BF16=jnp.bfloat16
SCALE=HD**-0.5

def nn(a,b): return lax.dot_general(a,b,(((1,),(0,)),((),())),preferred_element_type=F32)
def nt(a,b): return lax.dot_general(a,b,(((1,),(1,)),((),())),preferred_element_type=F32)
def tn(a,b): return lax.dot_general(a,b,(((0,),(0,)),((),())),preferred_element_type=F32)

def tile_groups(t):
    out=[]
    for g in range(12):
        lo=max(GL*g-128*t,0); hi=min(GL*(g+1)-128*t,128)
        if lo<hi: out.append((g,lo,hi))
    return out

def window(w, b, x_scr,o_scr,gain,shift,wq,wk,wv,wkT,wvT,wp,bias_ref,
           fold_ref, s_scr,dp_scr,ph_scr,ds_scr,fold_scr, normed_scr,gq_scr,gk_scr,gv_scr,ctx_scr,up_scr,tail_scr,row7_scr,
           eye144, base):
    toks=pl.ds(pl.multiple_of(b*WTOK,WTOK),WTOK)
    x=x_scr[0,toks].astype(F32)
    u=x_scr[1,toks]
    mean=jnp.mean(x,axis=-1,keepdims=True)
    cen=x-mean
    inv=lax.rsqrt(jnp.mean(cen*cen,axis=-1,keepdims=True)+EPSILON)
    std=cen*inv
    normed=(std*gain+shift).astype(BF16)
    q=nn(normed,wq).astype(BF16)
    k=nn(normed,wk).astype(BF16)
    v=nn(normed,wv).astype(BF16)
    kT=nt(wkT,normed).astype(BF16)
    vT=nt(wvT,normed).astype(BF16)
    dctx=nt(u,wp).astype(BF16)
    lane_c=lax.broadcasted_iota(jnp.int32,(1,C),1)//HD
    def blocks(m):
        zero=jnp.zeros_like(m)
        parts=[jnp.where(lane_c==h,m,zero) for h in range(HEADS)]
        return jnp.concatenate(parts+[jnp.zeros((QP-HEADS*WTOK,C),BF16)],axis=0)
    qblk=blocks(q); dblk=blocks(dctx)
    s_scr[w]=nt(k,qblk)
    dp_scr[w]=nt(v,dblk)
    lane=lax.broadcasted_iota(jnp.int32,(24,128),1)
    acc={}
    for t in range(7):
        groups=tile_groups(t)
        rows=[]
        for zk in range(WZ):
            for j in range(3):
                tile=None
                for (g,lo,hi) in groups:
                    h,zq=g//2,g%2
                    shift_=(GL*g-128*t-24*(2-j))%128
                    piece=bias_ref[0,h,w,zq,zk]
                    if shift_: piece=pltpu.roll(piece,shift_,1)
                    tile=piece if tile is None else jnp.where(lane>=lo,piece,tile)
                if groups[-1][2]<128: tile=jnp.where(lane<groups[-1][2],tile,0.0)
                rows.append(tile)
        bias=jnp.concatenate(rows,axis=0)
        cols=slice(128*t,128*(t+1))
        s=s_scr[w,:,cols]*SCALE+bias
        m=jnp.max(s,axis=0,keepdims=True)
        e=jnp.exp(s-m)
        p=e*(1.0/jnp.sum(e,axis=0,keepdims=True))
        ph_scr[w,:,cols]=p.astype(BF16)
        dp=dp_scr[w,:,cols]
        ds=p*(dp-jnp.sum(p*dp,axis=0,keepdims=True))
        ds_scr[w,:,cols]=(ds*SCALE).astype(BF16)
        for zk in range(WZ):
            for (g,lo,hi) in groups:
                tot=None
                for j in range(3):
                    r0=zk*72+24*j
                    piece=ds[r0:r0+24]
                    if lo>0 or hi<128:
                        piece=jnp.where((lane>=lo)&(lane<hi),piece,0.0)
                    back=(-(GL*g-128*t-24*(2-j)))%128
                    if back: piece=pltpu.roll(piece,back,1)
                    tot=piece if tot is None else tot+piece
                h,zq=g//2,g%2
                if GL*g-128*t>=0:
                    fold_scr[w,h,zq,zk]=tot
                else:
                    fold_scr[w,h,zq,zk]+=tot
    for h in range(HEADS):
        for zq in range(WZ):
            for zk in range(WZ):
                f=fold_scr[w,h,zq,zk]
                lo_t=None; hi_t=None
                lane6=lax.broadcasted_iota(jnp.int32,(8,128),1)
                for dw in range(4):
                    part=jnp.concatenate([f[6*dw:6*dw+6],jnp.zeros((2,128),F32)],axis=0)
                    sh=18-6*dw
                    r=pltpu.roll(part,sh,1) if sh else part
                    a=jnp.where(lane6>=sh,r,0.0) if sh>8 else r
                    lo_t=a if lo_t is None else lo_t+a
                    if sh>8:
                        b=jnp.where(lane6<sh-8,r,0.0)
                        hi_t=b if hi_t is None else hi_t+b
                n=(h*WZ+zq)*WZ+zk
                fold_ref[0,w,24*(n//3)+7*(n%3):24*(n//3)+7*(n%3)+6]=lo_t[:6]
                tail_scr[w,8*n:8*n+8]=hi_t
    tail=tail_scr[w,pl.ds(0,24,stride=8),:]
    for hk in range(1,WLAT):
        tail=tail+pltpu.roll(tail_scr[w,pl.ds(hk,24,stride=8),:],10*hk,1)
    row7_scr[w]=tail
    for m in range(3):
        fold_ref[0,w,pl.ds(7*m+6,8,stride=24),:]=row7_scr[w,pl.ds(m,8,stride=3),:]
    ph=ph_scr[w]; dsc=ds_scr[w]
    ctxT=jnp.concatenate([nn(vT[32*h:32*h+32],ph[:,128*h:128*h+256])[:,16*h:16*h+WTOK] for h in range(HEADS)],axis=0).astype(BF16)
    dqT=jnp.concatenate([nn(kT[32*h:32*h+32],dsc[:,128*h:128*h+256])[:,16*h:16*h+WTOK] for h in range(HEADS)],axis=0).astype(BF16)
    ctx=nt(eye144,ctxT).astype(BF16)
    dq=nt(eye144,dqT).astype(BF16)
    dv=nn(ph,dblk).astype(BF16)
    dk=nn(dsc,qblk).astype(BF16)
    o_scr[0,toks]=(x+nn(ctx,wp)).astype(BF16)
    ng=nt(dq,wq)+nt(dk,wk)+nt(dv,wv)
    g=ng*gain
    br=inv*(g-jnp.mean(g,axis=-1,keepdims=True)-std*jnp.mean(g*std,axis=-1,keepdims=True))
    o_scr[1,toks]=(u.astype(F32)+br).astype(BF16)
    rows=pl.ds(base+w*WTOK,WTOK)
    normed_scr[rows]=normed; gq_scr[rows]=dq; gk_scr[rows]=dk; gv_scr[rows]=dv; ctx_scr[rows]=ctx; up_scr[rows]=u
    return jnp.sum(ng*std,axis=0,keepdims=True), jnp.sum(ng,axis=0,keepdims=True)

def kernel(tl_ref,tr_ref,bl_ref,br_ref,left_ref,right_ref,perm_ref,back_ref,
           gain_ref,shift_ref,wq_ref,wk_ref,wv_ref,wkT_ref,wvT_ref,wp_ref,bias_ref,
           otl_ref,otr_ref,obl_ref,obr_ref,oleft_ref,oright_ref,fold_ref,wgrad_ref,x_scr,o_scr,*scr):
    w_scr,ngrad_scr=scr[13:]
    a=pl.program_id(0); pair=pl.program_id(1)
    step=a*2+pair
    half=slice(0,WTOK); rest=slice(WTOK,2*WTOK)
    @pl.when((a==0)&(pair==0))
    def _():
        for s in range(2):
            t=jnp.concatenate([tl_ref[s],tr_ref[s],bl_ref[s],br_ref[s]],axis=0)
            x_scr[s]=nn(perm_ref[...],t).astype(BF16)
    @pl.when((a==1)&(pair==0))
    def _():
        for s in range(2):
            t=jnp.concatenate([left_ref[s,half],right_ref[s,half],left_ref[s,rest],right_ref[s,rest]],axis=0)
            x_scr[s]=nn(perm_ref[...],t).astype(BF16)
    eye=(lax.broadcasted_iota(jnp.int32,(WTOK,WTOK),0)==lax.broadcasted_iota(jnp.int32,(WTOK,WTOK),1)).astype(BF16)
    base=pl.multiple_of(step*2*WTOK,2*WTOK)
    gs=[]
    for w in range(2):
        gs.append(window(w,pair*2+w,x_scr,o_scr,gain_ref[...],shift_ref[...],wq_ref[...],wk_ref[...],wv_ref[...],wkT_ref[...],wvT_ref[...],wp_ref[...],bias_ref,
            fold_ref,*scr[:13],eye,base))
    @pl.when((a==0)&(pair==1))
    def _():
        for s in range(2):
            t=nn(back_ref[...],o_scr[s]).astype(BF16)
            for n,ref in enumerate((otl_ref,otr_ref,obl_ref,obr_ref)):
                ref[s]=t[WTOK*n:WTOK*(n+1)]
    @pl.when((a==1)&(pair==1))
    def _():
        for s in range(2):
            t=nn(back_ref[...],o_scr[s]).astype(BF16)
            oleft_ref[s,half]=t[:WTOK]; oright_ref[s,half]=t[WTOK:2*WTOK]
            oleft_ref[s,rest]=t[2*WTOK:3*WTOK]; oright_ref[s,rest]=t[3*WTOK:]
    both=jnp.concatenate([gs[0][0]+gs[1][0],gs[0][1]+gs[1][1],jnp.zeros((6,C),F32)],axis=0)
    @pl.when(step==0)
    def _(): ngrad_scr[...]=both
    @pl.when(step>0)
    def _(): ngrad_scr[...]+=both
    @pl.when(step==3)
    def _():
        normed_scr,gq_scr,gk_scr,gv_scr,ctx_scr,up_scr=scr[5:11]
        n=normed_scr[...]
        whole=jnp.concatenate([tn(n,gq_scr[...]),tn(n,gk_scr[...]),tn(n,gv_scr[...]),tn(ctx_scr[...],up_scr[...])],axis=1)
        for t in range(6):
            w_scr[C*t:C*(t+1)]=whole[:,128*t:128*(t+1)]
        for r in range(3):
            for t in range(6):
                m=r*6+t
                wgrad_ref[pl.ds((m//9)*64*16+m%9,64,stride=16),:]=w_scr[pl.ds(C*t+r,64,stride=3),:]
        ng=ngrad_scr[...]
        for half in range(2):
            wgrad_ref[pl.ds(half*64*16+9,64,stride=16),:]=jnp.broadcast_to(ng[half:half+1,:128],(64,128))
            wgrad_ref[pl.ds(half*64*16+10,64,stride=16),:]=jnp.broadcast_to(jnp.concatenate([ng[half:half+1,128:],jnp.zeros((1,64),F32)],axis=1),(64,128))

def token_order():
    hot=np.zeros((576,576),np.float32)
    for lev in range(8):
        for w in range(WLON):
            for h in range(WLAT):
                quad=h//3*2+w//6
                hot[(lev*WLON+w)*WLAT+h,quad*WTOK+h%3*48+w%6*8+(lev-1)%8]=1.0
    return hot

def attend(parts,gain,shift,wqkv,wp,vtab):
    wq,wk,wv=wqkv[:,:C],wqkv[:,C:2*C],wqkv[:,2*C:]
    full=lambda *s: pl.BlockSpec(s,lambda i,j:(0,)*len(s))
    tok=8*WTOK
    hot=token_order()
    grids=[full(*p.shape) for p in parts]
    return pl.pallas_call(
        kernel,
        grid=(2,2),
        in_specs=grids+[full(4*WTOK,4*WTOK)]*2+[full(1,C),full(1,C)]+[full(C,C)]*6+[pl.BlockSpec((1,HEADS,2,WZ,WZ,24,128),lambda i,j:(i,0,j,0,0,0,0))],
        out_specs=grids+[pl.BlockSpec((1,2,192,128),lambda i,j:(i,j,0,0)),full(2*64*16,128)],
        out_shape=[jax.ShapeDtypeStruct(p.shape,BF16) for p in parts]+[
                   jax.ShapeDtypeStruct((2,4,192,128),F32),
                   jax.ShapeDtypeStruct((2*64*16,128),F32)],
        scratch_shapes=[pltpu.VMEM((2,4*WTOK,C),BF16),pltpu.VMEM((2,4*WTOK,C),BF16),
                        pltpu.VMEM((2,WTOK,QP),F32),pltpu.VMEM((2,WTOK,QP),F32),pltpu.VMEM((2,WTOK,QP),BF16),pltpu.VMEM((2,WTOK,QP),BF16),
                        pltpu.VMEM((2,HEADS,WZ,WZ,24,128),F32)]+[pltpu.VMEM((tok,C),BF16)]*6
                       +[pltpu.VMEM((2,192,128),F32),pltpu.VMEM((2,24,128),F32)]+[pltpu.VMEM((6*C,128),F32),pltpu.VMEM((8,C),F32)],
        compiler_params=pltpu.CompilerParams(dimension_semantics=("arbitrary","arbitrary"),vmem_limit_bytes=32*1024*1024),
        cost_estimate=pl.CostEstimate(flops=6*10**9,bytes_accessed=8000000,transcendentals=10**6),
        name="attend",
    )(*parts,jnp.asarray(hot,BF16),jnp.asarray(hot.T,BF16),gain.reshape(1,C),shift.reshape(1,C),wq,wk,wv,wk.T,wv.T,wp,vtab)

def table_order():
    hot=np.zeros((828,896),np.float32)
    for hq in range(WLAT):
        for hk in range(WLAT):
            for o in range(23):
                i=o*WLAT+hq
                hot[(hq*WLAT+hk)*23+o,128*hk+i if i<128 else 768+10*hk+i-128]=1.0
    return hot

def table_kernel(lat_ref,t_ref,hot_ref,out_ref):
    rows=2*HEADS*4
    row=lax.broadcasted_iota(jnp.int32,(rows,128),0)
    lane=lax.broadcasted_iota(jnp.int32,(rows,128),1)
    low=lane%WLAT<WLAT//2
    edge=(row<rows//2)&(lat_ref[0]==0)
    bottom=row%4==0
    hot=hot_ref[...]
    for zz in range(4):
        t=t_ref[:,828*zz:828*(zz+1)]
        hi=t.astype(BF16); rest=t-hi.astype(F32)
        mid=rest.astype(BF16); lo=(rest-mid.astype(F32)).astype(BF16)
        v=nn(jnp.concatenate([hi,mid,lo],axis=0),hot)
        v=v[:rows]+v[rows:2*rows]+v[2*rows:]
        tail=v[:,768:896]
        for hk in range(WLAT):
            main=v[:,128*hk:128*(hk+1)]
            cut=edge&(low!=(hk<WLAT//2))
            if zz in (1,2): cut=cut|bottom
            for dw in range(4):
                s=18-6*dw
                r=pltpu.roll(main,128-s,1) if s else main
                if s>8:
                    r=jnp.where(lane>=128-s,pltpu.roll(tail,(128-s-10*hk)%128,1),r)
                out_ref[pl.ds(zz*24+dw*WLAT+hk,rows,stride=96),:]=jnp.where(cut,MASKED,r)

def spread_table(earth_bias, lat):
    flat=earth_bias.transpose(0,2,1,3).reshape(48,POSITIONS)
    whole=pl.BlockSpec(memory_space=pltpu.VMEM)
    out=pl.pallas_call(
        table_kernel,
        in_specs=[pl.BlockSpec(memory_space=pltpu.SMEM),whole,whole],
        out_specs=whole,
        out_shape=jax.ShapeDtypeStruct((48*96,128),F32),
        compiler_params=pltpu.CompilerParams(vmem_limit_bytes=16*1024*1024),
        cost_estimate=pl.CostEstimate(flops=2*576*828*896,bytes_accessed=5000000,transcendentals=0),
        name="table",
    )(jnp.full((1,),lat,jnp.int32),flat,jnp.asarray(table_order(),BF16))
    return out.reshape(2,HEADS,4,WZ,WZ,24,128)

def unfold_grad(g):
    n=g.shape[0]
    v=jnp.concatenate([g[:,:6],g[:,6,:60].reshape(n,6,10)],axis=-1)
    return v.reshape(n,WLAT,23,WLAT).transpose(0,3,1,2).reshape(n,828)

LON = ("xl", "y", "z")
LAT = ("xh", "c")
ZWIN = 4
GRAD_SCALE = 1.0 / math.sqrt(294912)


def along(block, axis, distance):
    size = lax.axis_size(axis)
    return lax.ppermute(block, axis, [(i, (i + distance) % size) for i in range(size)])


def across(block, lon_step, lat_step):
    lon, lat = lax.axis_size(LON), lax.axis_size(LAT)
    route = [
        (i * lat + j, (i + lon_step) % lon * lat + (j + lat_step) % lat)
        for i in range(lon)
        for j in range(lat)
    ]
    return lax.ppermute(block, LON + LAT, route)


def pack_kernel(x_ref, u_ref, *outs):
    west, east = slice(0, WLON // 2), slice(WLON // 2, WLON)
    upper, middle, lower = slice(0, WLAT // 2), slice(WLAT // 2, 3 * WLAT // 2), slice(3 * WLAT // 2, 2 * WLAT)
    places = ((middle, west), (upper, east), (lower, east), (lower, west), (upper, west), (middle, east))
    for ref, (rows, cols) in zip(outs, places):
        ref[0] = x_ref[rows, cols]
        ref[1] = u_ref[rows, cols]


def pack(x, u):
    whole = pl.BlockSpec(memory_space=pltpu.VMEM)
    half = WLON // 2
    shapes = [(2, rows, half, 8, C) for rows in (6, 3, 3, 3, 3, 6)]
    return pl.pallas_call(
        pack_kernel,
        in_specs=[whole, whole],
        out_specs=[whole] * 6,
        out_shape=[jax.ShapeDtypeStruct(s, BF16) for s in shapes],
        compiler_params=pltpu.CompilerParams(vmem_limit_bytes=8 * 1024 * 1024),
        name="pack",
    )(x, u)


def on_device(air_state, cotangent, norm_gain, norm_shift, qkv_weight, proj_weight, earth_bias):
    half = WLON // 2
    sent_right, sent_bottom, sent_corner, sent_above, own_upper, own_middle = [
        p.reshape(2, -1, C) for p in pack(air_state.transpose(1, 2, 0, 3), cotangent.transpose(1, 2, 0, 3))
    ]
    right = across(sent_right, -1, 0)
    bottom = across(sent_bottom, 1, 0)
    corner = across(sent_corner, 1, 1)
    above = across(sent_above, 0, 1)
    parts = [corner, above, bottom, own_upper, own_middle, right]
    table = spread_table(earth_bias, lax.axis_index(LAT))
    *outs, fold, wgrad = attend(parts, norm_gain, norm_shift, qkv_weight, proj_weight, table)
    wgrad = wgrad.reshape(2, 64, 16, 128)[:, :, :11].astype(BF16)

    corner, above, bottom, own_upper, own_middle, right = outs
    right = across(right, 1, 0)
    bottom = across(bottom, -1, 0)
    corner = across(corner, -1, -1)
    above = across(above, 0, -1)

    core = lax.axis_index("c")
    kept = lax.dynamic_index_in_dim(wgrad, core, 0, keepdims=False)
    other = along(lax.dynamic_index_in_dim(wgrad, 1 - core, 0, keepdims=False), "c", 1)
    wpart = (kept.astype(F32) + other.astype(F32)).astype(BF16)
    payload = jnp.concatenate((fold.reshape(64, 24, 128)[:, :21].astype(BF16), wpart), axis=1)
    parts = lax.all_to_all(payload, LON, 0, 0, tiled=True)
    mine = jnp.sum(parts.astype(F32), axis=0)
    wsum = mine[21:]
    wsum = (wsum + along(wsum, "xh", 1)) * GRAD_SCALE
    bsum = unfold_grad(mine[:21].reshape(3, 7, 128)).reshape(-1)
    bsum = jnp.pad(bsum, (0, 20 * 128 - bsum.shape[0])).reshape(20, 128)
    shard = jnp.concatenate((bsum, wsum), axis=0).astype(BF16)
    shard = jnp.pad(shard, ((0, 1), (0, 0)))
    shard, right, bottom, corner, above = lax.optimization_barrier((shard, right, bottom, corner, above))
    spread = lax.all_to_all(jnp.broadcast_to(shard, (64,) + shard.shape), LON, 0, 0, tiled=True)
    bias_grad = spread[:, :20].reshape(64, 2560)[:, :2484].reshape(2, ZWIN, HEADS, POSITIONS)
    whalf = spread[:, 20:29]
    nhalf = wsum[9:11]
    wother = along(whalf, "c", 1)
    nother = along(nhalf, "c", 1)
    first = core == 0
    w0 = jnp.where(first, whalf, wother)
    w1 = jnp.where(first, wother, whalf)
    wall = jnp.concatenate((w0, w1), axis=1).reshape(C, 4 * C).astype(F32)
    gain_grad = jnp.where(first, nhalf, nother).reshape(256)[:C]
    shift_grad = jnp.where(first, nother, nhalf).reshape(256)[:C]

    def joined(left, right):
        return jnp.concatenate([t.reshape(2, -1, half, 8, C) for t in (left, right)], axis=2)

    grid = jnp.concatenate((joined(own_upper, bottom), joined(right, own_middle), joined(above, corner)), axis=1)
    both = grid.transpose(0, 3, 1, 2, 4)

    return both[0], both[1], wall[:, : 3 * C], wall[:, 3 * C :], gain_grad, shift_grad, bias_grad


def solution(mesh):
    fine = Mesh(mesh.devices.reshape(2, 4, 8, 2, 2), LON + LAT)
    token = P(None, LAT, LON, None)
    table = P(LAT, None, None, None)
    return jax.shard_map(
        on_device,
        mesh=fine,
        in_specs=(token, token, P(), P(), P(), P(), table),
        out_specs=(token, token, P(), P(), P(), P(), table),
        check_vma=False,
    )
```

profile of v0, /device:TPU:1, one launch (start us, length us, event | category | flops | bytes accessed | tf_op | source)
XLA Modules:
  0.0 109.2 jit_solution(10481440748411752413)
XLA Ops:
  0.6 1.1 copy-done.1
  1.7 1.1 copy-done.2
  4.2 9.8 %collective-permute-start.3 = (bf16[2,288,192]{2,1,0:T(8,128)(2,1)S(1)}, bf16[2,288,192]{2,1,0:T(8,128)(2,1)S(1)}, u32[]{:S(2)}, u32[]{:S(2)}) collective-permute-start(bf16[2,288,192]{2,1,0:T(8,128)(2,1)S(1)} %bitcast.59), channel_id=1, source_target_pairs={{0,252},{1,253},{2,254},{3,255},{4,0},{5,1},{6,2},{7,3},{8,4},{9,5... | collective-permute-start | bytes 663560 | tf_op jit(solution)/shard_map/ppermute | solution.py:299
  14.0 3.3 %collective-permute-start.1 = (bf16[2,144,192]{2,1,0:T(8,128)(2,1)}, bf16[2,144,192]{2,1,0:T(8,128)(2,1)}, u32[]{:S(2)}, u32[]{:S(2)}) collective-permute-start(bf16[2,144,192]{2,1,0:T(8,128)(2,1)} %bitcast.3), channel_id=1, source_target_pairs={{0,1},{1,2},{2,3},{3,0},{4,5},{5,6},{6,7},{7,4},{8,9},{9,10},{10,1... | collective-permute-start | bytes 331784 | tf_op jit(solution)/shard_map/ppermute | solution.py:299
  17.4 1.3 %reshape.106.t_ref = f32[48,3312]{1,0:T(8,128)S(1)} reshape(f32[2,6,4,3312]{3,2,1,0:T(4,128)} %bitcast.68) | data formatting | bytes 1271808 | tf_op jit(solution)/shard_map/reshape | solution.py:263
  19.0 2.7 %table.1 = f32[4608,128]{1,0:T(8,128)S(1)} custom-call(s32[1]{0:T(128)} %bitcast.12.lat_ref, f32[48,3312]{1,0:T(8,128)S(1)} %reshape.106.t_ref, bf16[828,896]{1,0:T(8,128)(2,1)S(1)} %copy-done), custom_call_target="tpu_custom_call" | custom-call | flops 854654976 | bytes 5000000 | tf_op jit(solution)/shard_map/table/pallas_call | solution.py:265
  21.7 2.3 %collective-permute-done.tl_ref = bf16[2,144,192]{2,1,0:T(8,128)(2,1)} collective-permute-done((bf16[2,144,192]{2,1,0:T(8,128)(2,1)}, bf16[2,144,192]{2,1,0:T(8,128)(2,1)}, u32[]{:S(2)}, u32[]{:S(2)}) %collective-permute-start) | collective-permute-done | bytes 110624 | tf_op jit(solution)/shard_map/ppermute | solution.py:299
  24.1 4.1 %collective-permute-done.2.bl_ref = bf16[2,144,192]{2,1,0:T(8,128)(2,1)} collective-permute-done((bf16[2,144,192]{2,1,0:T(8,128)(2,1)}, bf16[2,144,192]{2,1,0:T(8,128)(2,1)}, u32[]{:S(2)}, u32[]{:S(2)}) %collective-permute-start.2) | collective-permute-done | bytes 110624 | tf_op jit(solution)/shard_map/ppermute | solution.py:299
  28.2 18.0 %attend.1 = (bf16[2,144,192]{2,1,0:T(8,128)(2,1)S(1)}, bf16[2,144,192]{2,1,0:T(8,128)(2,1)S(1)}, bf16[2,144,192]{2,1,0:T(8,128)(2,1)S(1)}, bf16[2,144,192]{2,1,0...) custom-call(bf16[2,144,192]{2,1,0:T(8,128)(2,1)} %collective-permute, ...), custom_call_target="tpu_custom_call" | custom-call | flops 6000000000 | bytes 8000000 | tf_op jit(solution)/shard_map/attend/pallas_call | solution.py:210
  46.6 1.5 %collective-permute-done.4 = bf16[64,11,128]{2,1,0:T(8,128)(2,1)S(1)} collective-permute-done((bf16[64,11,128]{2,1,0:T(8,128)(2,1)S(1)}, bf16[64,11,128]{2,1,0:T(8,128)(2,1)S(1)}, u32[]{:S(2)}, u32[]{:S(2)}) %collective-permute-start.4) | collective-permute-done | bytes 180256 | tf_op jit(solution)/shard_map/ppermute | solution.py:289
  48.1 0.9 pad_maximum_fusion
  49.0 4.6 %all-to-all-start = ((bf16[64,32,128]{2,1,0:T(8,128)(2,1)}), bf16[64,32,128]{2,1,0:T(8,128)(2,1)S(1)}, u32[]{:S(2)}, u32[]{:S(2)}) async-start(bf16[64,32,128]{2,1,0:T(8,128)(2,1)} %pad_maximum_fusion), calls=%async_computation | async-start | bytes 1048576 | tf_op jit(solution)/shard_map/all_to_all | solution.py:350
  53.7 1.0 collective-permute-start.6
  54.7 4.8 %collective-permute-start.7 = (bf16[2,144,192]{2,1,0:T(8,128)(2,1)S(1)}, bf16[2,144,192]{2,1,0:T(8,128)(2,1)S(1)}, u32[]{:S(2)}, u32[]{:S(2)}) collective-permute-start(bf16[2,144,192]{2,1,0:T(8,128)(2,1)S(1)} %get-tuple-element.36), channel_id=1, source_target_pairs={{0,252},{1,253},{2,254},{3,255},{4,0},{5,1},{6,2},{7,3},{8,4},{9,5... | collective-permute-start | bytes 331784 | tf_op jit(solution)/shard_map/ppermute | solution.py:299
  59.4 2.2 %collective-permute-start.8 = (bf16[2,144,192]{2,1,0:T(8,128)(2,1)S(1)}, bf16[2,144,192]{2,1,0:T(8,128)(2,1)S(1)}, u32[]{:S(2)}, u32[]{:S(2)}) collective-permute-start(bf16[2,144,192]{2,1,0:T(8,128)(2,1)S(1)} %get-tuple-element.37), channel_id=1, source_target_pairs={{0,255},{1,252},{2,253},{3,254},{4,3},{5,0},{6,1},{7,2},{8,7},{9,4... | collective-permute-start | bytes 331784 | tf_op jit(solution)/shard_map/ppermute | solution.py:299
  62.3 9.7 %all-to-all-done = bf16[64,32,128]{2,1,0:T(8,128)(2,1)S(1)} async-done(((bf16[64,32,128]{2,1,0:T(8,128)(2,1)}), bf16[64,32,128]{2,1,0:T(8,128)(2,1)S(1)}, u32[]{:S(2)}, u32[]{:S(2)}) %all-to-all-start) | async-done | bytes 524320 | tf_op jit(solution)/shard_map/all_to_all | solution.py:350
  72.1 2.0 %collective-permute-start.5 = (f32[11,128]{1,0:T(8,128)S(1)}, f32[11,128]{1,0:T(8,128)S(1)}, u32[]{:S(2)}, u32[]{:S(2)}) collective-permute-start(f32[11,128]{1,0:T(8,128)S(1)} %slice.85), channel_id=1, source_target_pairs={{0,2},{2,0},{1,3},{3,1},{4,6},{6,4},{5,7},{7,5},{8,10},{10,8},{9,1... | collective-permute-start | bytes 16904 | tf_op jit(solution)/shard_map/ppermute | solution.py:289
  74.9 1.6 %collective-permute-done.5 = f32[11,128]{1,0:T(8,128)S(1)} collective-permute-done((f32[11,128]{1,0:T(8,128)S(1)}, f32[11,128]{1,0:T(8,128)S(1)}, u32[]{:S(2)}, u32[]{:S(2)}) %collective-permute-start.5) | collective-permute-done | bytes 5664 | tf_op jit(solution)/shard_map/ppermute | solution.py:289
  76.6 2.0 %collective-permute-done.6 = bf16[2,288,192]{2,1,0:T(8,128)(2,1)S(1)} collective-permute-done((bf16[2,288,192]{2,1,0:T(8,128)(2,1)S(1)}, bf16[2,288,192]{2,1,0:T(8,128)(2,1)S(1)}, u32[]{:S(2)}, u32[]{:S(2)}) %collective-permute-start.6) | collective-permute-done | bytes 221216 | tf_op jit(solution)/shard_map/ppermute | solution.py:299
  78.6 0.9 broadcast_in_dim.7
  79.5 5.9 %all-to-all-start.1 = ((bf16[64,32,128]{2,1,0:T(8,128)(2,1)}), bf16[64,32,128]{2,1,0:T(8,128)(2,1)S(1)}, u32[]{:S(2)}, u32[]{:S(2)}) async-start(bf16[64,32,128]{2,1,0:T(8,128)(2,1)} %broadcast_in_dim.7), calls=%async_computation.1 | async-start | bytes 1048576 | tf_op jit(solution)/shard_map/all_to_all | solution.py:359
  85.8 1.1 slice_bitcast_fusion
  86.8 16.9 %all-to-all-done.1 = bf16[64,32,128]{2,1,0:T(8,128)(2,1)S(1)} async-done(((bf16[64,32,128]{2,1,0:T(8,128)(2,1)}), bf16[64,32,128]{2,1,0:T(8,128)(2,1)S(1)}, u32[]{:S(2)}, u32[]{:S(2)}) %all-to-all-start.1) | async-done | bytes 524320 | tf_op jit(solution)/shard_map/all_to_all | solution.py:359
  103.8 1.3 %collective-permute-start.10 = (bf16[64,9,128]{2,1,0:T(8,128)(2,1)S(1)}, bf16[64,9,128]{2,1,0:T(8,128)(2,1)S(1)}, u32[]{:S(2)}, u32[]{:S(2)}) collective-permute-start(bf16[64,9,128]{2,1,0:T(8,128)(2,1)S(1)} %slice.88), channel_id=1, source_target_pairs={{0,1},{1,0},{2,3},{3,2},{4,5},{5,4},{6,7},{7,6},{8,9},{9,8},{10,11... | collective-permute-start | bytes 442376 | tf_op jit(solution)/shard_map/ppermute | solution.py:289
  (66 shorter events, 8.4 us)
Async XLA Ops:
  0.6 1.1 copy-start.1
  1.7 1.1 copy-start.2
  2.8 14.5 %copy-start.10 = (bf16[192,576]{1,0:T(8,128)(2,1)S(1)}, bf16[192,576]{1,0:T(8,128)(2,1)}, u32[]{:S(2)}) copy-start(bf16[192,576]{1,0:T(8,128)(2,1)} %param.14) | copy-start | bytes 663556
  4.2 14.7 %copy-start = (bf16[828,896]{1,0:T(8,128)(2,1)S(1)}, bf16[828,896]{1,0:T(8,128)(2,1)}, u32[]{:S(2)}) copy-start(bf16[828,896]{1,0:T(8,128)(2,1)} %constant.34.clone.hot_ref) | copy-start | bytes 4451332
  4.2 23.9 %collective-permute-start.3 = (bf16[2,288,192]{2,1,0:T(8,128)(2,1)S(1)}, bf16[2,288,192]{2,1,0:T(8,128)(2,1)S(1)}, u32[]{:S(2)}, u32[]{:S(2)}) collective-permute-start(bf16[2,288,192]{2,1,0:T(8,128)(2,1)S(1)} %bitcast.59), channel_id=1, source_target_pairs={{0,252},{1,253},{2,254},{3,255},{4,0},{5,1},{6,2},{7,3},{8,4},{9,5... | collective-permute-start | bytes 663560 | tf_op jit(solution)/shard_map/ppermute | solution.py:299
  14.0 10.1 %collective-permute-start = (bf16[2,144,192]{2,1,0:T(8,128)(2,1)}, bf16[2,144,192]{2,1,0:T(8,128)(2,1)}, u32[]{:S(2)}, u32[]{:S(2)}) collective-permute-start(bf16[2,144,192]{2,1,0:T(8,128)(2,1)} %bitcast.2), channel_id=1, source_target_pairs={{0,5},{1,6},{2,7},{3,4},{4,9},{5,10},{6,11},{7,8},{8,13},{9,14},{1... | collective-permute-start | bytes 331784 | tf_op jit(solution)/shard_map/ppermute | solution.py:299
  14.0 10.1 %collective-permute-start.1 = (bf16[2,144,192]{2,1,0:T(8,128)(2,1)}, bf16[2,144,192]{2,1,0:T(8,128)(2,1)}, u32[]{:S(2)}, u32[]{:S(2)}) collective-permute-start(bf16[2,144,192]{2,1,0:T(8,128)(2,1)} %bitcast.3), channel_id=1, source_target_pairs={{0,1},{1,2},{2,3},{3,0},{4,5},{5,6},{6,7},{7,4},{8,9},{9,10},{10,1... | collective-permute-start | bytes 331784 | tf_op jit(solution)/shard_map/ppermute | solution.py:299
  17.3 10.8 %collective-permute-start.2 = (bf16[2,144,192]{2,1,0:T(8,128)(2,1)}, bf16[2,144,192]{2,1,0:T(8,128)(2,1)}, u32[]{:S(2)}, u32[]{:S(2)}) collective-permute-start(bf16[2,144,192]{2,1,0:T(8,128)(2,1)} %bitcast.4), channel_id=1, source_target_pairs={{0,4},{1,5},{2,6},{3,7},{4,8},{5,9},{6,10},{7,11},{8,12},{9,13},{1... | collective-permute-start | bytes 331784 | tf_op jit(solution)/shard_map/ppermute | solution.py:299
  18.9 9.2 %copy-start.4 = (bf16[2,3,6,8,192]{4,3,2,1,0:T(8,128)(2,1)S(1)}, bf16[2,3,6,8,192]{4,3,2,1,0:T(8,128)(2,1)}, u32[]{:S(2)}) copy-start(bf16[2,3,6,8,192]{4,3,2,1,0:T(8,128)(2,1)} %copy-done.3) | copy-start | bytes 331780
  19.0 9.2 %copy-start.5 = (bf16[192,192]{1,0:T(8,128)(2,1)S(1)}, bf16[192,192]{1,0:T(8,128)(2,1)}, u32[]{:S(2)}) copy-start(bf16[192,192]{1,0:T(8,128)(2,1)} %wp_ref.1) | copy-start | bytes 221188
  19.0 9.2 %copy-start.6 = (f32[192]{0:T(256)S(1)}, f32[192]{0:T(256)}, u32[]{:S(2)}) copy-start(f32[192]{0:T(256)} %param.12) | copy-start | bytes 2308
  19.0 9.2 %copy-start.7 = (f32[192]{0:T(256)S(1)}, f32[192]{0:T(256)}, u32[]{:S(2)}) copy-start(f32[192]{0:T(256)} %param.13) | copy-start | bytes 2308
  19.0 9.2 %copy-start.8 = (bf16[576,576]{1,0:T(8,128)(2,1)S(1)}, bf16[576,576]{1,0:T(8,128)(2,1)}, u32[]{:S(2)}) copy-start(bf16[576,576]{1,0:T(8,128)(2,1)} %constant.35.clone.perm_ref) | copy-start | bytes 1990660
  19.0 9.2 %copy-start.9 = (bf16[576,576]{1,0:T(8,128)(2,1)S(1)}, bf16[576,576]{1,0:T(8,128)(2,1)}, u32[]{:S(2)}) copy-start(bf16[576,576]{1,0:T(8,128)(2,1)} %constant.36.clone.back_ref) | copy-start | bytes 1990660
  46.2 1.8 %collective-permute-start.4 = (bf16[64,11,128]{2,1,0:T(8,128)(2,1)S(1)}, bf16[64,11,128]{2,1,0:T(8,128)(2,1)S(1)}, u32[]{:S(2)}, u32[]{:S(2)}) collective-permute-start(bf16[64,11,128]{2,1,0:T(8,128)(2,1)S(1)} %dynamic-slice_bitcast_fusion), channel_id=1, source_target_pairs={{0,1},{1,0},{2,3},{3,2},{4,5},{5,4},{6,7},{7,6},{8,9},{9,8},{10,11... | collective-permute-start | bytes 540680 | tf_op jit(solution)/shard_map/ppermute | solution.py:289
  49.0 23.0 %all-to-all-start = ((bf16[64,32,128]{2,1,0:T(8,128)(2,1)}), bf16[64,32,128]{2,1,0:T(8,128)(2,1)S(1)}, u32[]{:S(2)}, u32[]{:S(2)}) async-start(bf16[64,32,128]{2,1,0:T(8,128)(2,1)} %pad_maximum_fusion), calls=%async_computation | async-start | bytes 1048576 | tf_op jit(solution)/shard_map/all_to_all | solution.py:350
  53.7 24.9 %collective-permute-start.6 = (bf16[2,288,192]{2,1,0:T(8,128)(2,1)S(1)}, bf16[2,288,192]{2,1,0:T(8,128)(2,1)S(1)}, u32[]{:S(2)}, u32[]{:S(2)}) collective-permute-start(bf16[2,288,192]{2,1,0:T(8,128)(2,1)S(1)} %get-tuple-element.35), channel_id=1, source_target_pairs={{0,4},{1,5},{2,6},{3,7},{4,8},{5,9},{6,10},{7,11},{8,12},{9,13},{1... | collective-permute-start | bytes 663560 | tf_op jit(solution)/shard_map/ppermute | solution.py:299
  54.7 21.9 %collective-permute-start.7 = (bf16[2,144,192]{2,1,0:T(8,128)(2,1)S(1)}, bf16[2,144,192]{2,1,0:T(8,128)(2,1)S(1)}, u32[]{:S(2)}, u32[]{:S(2)}) collective-permute-start(bf16[2,144,192]{2,1,0:T(8,128)(2,1)S(1)} %get-tuple-element.36), channel_id=1, source_target_pairs={{0,252},{1,253},{2,254},{3,255},{4,0},{5,1},{6,2},{7,3},{8,4},{9,5... | collective-permute-start | bytes 331784 | tf_op jit(solution)/shard_map/ppermute | solution.py:299
  59.4 17.1 %collective-permute-start.8 = (bf16[2,144,192]{2,1,0:T(8,128)(2,1)S(1)}, bf16[2,144,192]{2,1,0:T(8,128)(2,1)S(1)}, u32[]{:S(2)}, u32[]{:S(2)}) collective-permute-start(bf16[2,144,192]{2,1,0:T(8,128)(2,1)S(1)} %get-tuple-element.37), channel_id=1, source_target_pairs={{0,255},{1,252},{2,253},{3,254},{4,3},{5,0},{6,1},{7,2},{8,7},{9,4... | collective-permute-start | bytes 331784 | tf_op jit(solution)/shard_map/ppermute | solution.py:299
  61.6 14.9 %collective-permute-start.9 = (bf16[2,144,192]{2,1,0:T(8,128)(2,1)S(1)}, bf16[2,144,192]{2,1,0:T(8,128)(2,1)S(1)}, u32[]{:S(2)}, u32[]{:S(2)}) collective-permute-start(bf16[2,144,192]{2,1,0:T(8,128)(2,1)S(1)} %get-tuple-element.38), channel_id=1, source_target_pairs={{0,3},{1,0},{2,1},{3,2},{4,7},{5,4},{6,5},{7,6},{8,11},{9,8},{10,9... | collective-permute-start | bytes 331784 | tf_op jit(solution)/shard_map/ppermute | solution.py:299
  72.1 4.4 %collective-permute-start.5 = (f32[11,128]{1,0:T(8,128)S(1)}, f32[11,128]{1,0:T(8,128)S(1)}, u32[]{:S(2)}, u32[]{:S(2)}) collective-permute-start(f32[11,128]{1,0:T(8,128)S(1)} %slice.85), channel_id=1, source_target_pairs={{0,2},{2,0},{1,3},{3,1},{4,6},{6,4},{5,7},{7,5},{8,10},{10,8},{9,1... | collective-permute-start | bytes 16904 | tf_op jit(solution)/shard_map/ppermute | solution.py:289
  79.5 24.2 %all-to-all-start.1 = ((bf16[64,32,128]{2,1,0:T(8,128)(2,1)}), bf16[64,32,128]{2,1,0:T(8,128)(2,1)S(1)}, u32[]{:S(2)}, u32[]{:S(2)}) async-start(bf16[64,32,128]{2,1,0:T(8,128)(2,1)} %broadcast_in_dim.7), calls=%async_computation.1 | async-start | bytes 1048576 | tf_op jit(solution)/shard_map/all_to_all | solution.py:359
  85.4 19.7 %collective-permute-start.11 = (f32[2,128]{1,0:T(2,128)S(1)}, f32[2,128]{1,0:T(2,128)S(1)}, u32[]{:S(2)}, u32[]{:S(2)}) collective-permute-start(f32[2,128]{1,0:T(2,128)S(1)} %slice.91), channel_id=1, source_target_pairs={{0,1},{1,0},{2,3},{3,2},{4,5},{5,4},{6,7},{7,6},{8,9},{9,8},{10,11... | collective-permute-start | bytes 3080 | tf_op jit(solution)/shard_map/ppermute | solution.py:289
  103.8 3.5 %collective-permute-start.10 = (bf16[64,9,128]{2,1,0:T(8,128)(2,1)S(1)}, bf16[64,9,128]{2,1,0:T(8,128)(2,1)S(1)}, u32[]{:S(2)}, u32[]{:S(2)}) collective-permute-start(bf16[64,9,128]{2,1,0:T(8,128)(2,1)S(1)} %slice.88), channel_id=1, source_target_pairs={{0,1},{1,0},{2,3},{3,2},{4,5},{5,4},{6,7},{7,6},{8,9},{9,8},{10,11... | collective-permute-start | bytes 442376 | tf_op jit(solution)/shard_map/ppermute | solution.py:289
  (1 other events, 0.7 us)
where the time goes:
time: 110 us; the launch traced here: 109 us
  waiting for transfers between devices  38.1 us (35%)
  starting transfers between devices  35.8 us (33%)
  Pallas kernels  21.4 us (19%)
  local copies, waits for them, and re-layouts  10.6 us (10%)
  other arithmetic  2.26 us (2%)
    ppermute x8, starting transfers between devices, across(): return lax.ppermute(block, LON + LAT, route)  21.7 us
    pallas_call x1, Pallas kernels, attend(): pl.pallas_call(kernel, grid=(2, 2), in_specs=grids + [full(4 * WTOK, 4 *...  18 us
    all_to_all x1, waiting for transfers between devices, on_device(): lax.all_to_all(jnp.broadcast_to(shard, (64,) + shard.shape), LON, 0, 0, t...  16.9 us
    all_to_all x1, waiting for transfers between devices, on_device(): parts = lax.all_to_all(payload, LON, 0, 0, tiled=True)  9.72 us
    ppermute x8, waiting for transfers between devices, across(): return lax.ppermute(block, LON + LAT, route)  8.47 us
    all_to_all x1, starting transfers between devices, on_device(): lax.all_to_all(jnp.broadcast_to(shard, (64,) + shard.shape), LON, 0, 0, t...  5.89 us
    all_to_all x1, starting transfers between devices, on_device(): parts = lax.all_to_all(payload, LON, 0, 0, tiled=True)  4.63 us
    unnamed x26, local copies, waits for them, and re-layouts  3.92 us
  transfers between devices with their start and end apart: 14, of which 7 were waited for; matrix products, arithmetic and copies ran while one was open for 6% of the time, Pallas kernels for 2%

commit v1 on v0

--- a/solution.py
+++ b/solution.py
@@ -13,6 +13,7 @@
 C=192; HD=32
 EPSILON=1e-5
 MASKED=-1e30
+NW=4
 QP=896
 GL=72
 F32=jnp.float32; BF16=jnp.bfloat16
@@ -31,7 +32,7 @@
 
 def window(w, b, x_scr,o_scr,gain,shift,wq,wk,wv,wkT,wvT,wp,bias_ref,
            fold_ref, s_scr,dp_scr,ph_scr,ds_scr,fold_scr, normed_scr,gq_scr,gk_scr,gv_scr,ctx_scr,up_scr,tail_scr,row7_scr,
-           eye144, base):
+           eye144, base, result):
     toks=pl.ds(pl.multiple_of(b*WTOK,WTOK),WTOK)
     x=x_scr[0,toks].astype(F32)
     u=x_scr[1,toks]
@@ -46,6 +47,7 @@
     kT=nt(wkT,normed).astype(BF16)
     vT=nt(wvT,normed).astype(BF16)
     dctx=nt(u,wp).astype(BF16)
+    yield
     lane_c=lax.broadcasted_iota(jnp.int32,(1,C),1)//HD
     def blocks(m):
         zero=jnp.zeros_like(m)
@@ -54,9 +56,10 @@
     qblk=blocks(q); dblk=blocks(dctx)
     s_scr[w]=nt(k,qblk)
     dp_scr[w]=nt(v,dblk)
+    yield
     lane=lax.broadcasted_iota(jnp.int32,(24,128),1)
-    acc={}
     for t in range(7):
+        yield
         groups=tile_groups(t)
         rows=[]
         for zk in range(WZ):
@@ -96,6 +99,7 @@
                     fold_scr[w,h,zq,zk]=tot
                 else:
                     fold_scr[w,h,zq,zk]+=tot
+    yield
     for h in range(HEADS):
         for zq in range(WZ):
             for zk in range(WZ):
@@ -120,28 +124,32 @@
     row7_scr[w]=tail
     for m in range(3):
         fold_ref[0,w,pl.ds(7*m+6,8,stride=24),:]=row7_scr[w,pl.ds(m,8,stride=3),:]
+    yield
     ph=ph_scr[w]; dsc=ds_scr[w]
     ctxT=jnp.concatenate([nn(vT[32*h:32*h+32],ph[:,128*h:128*h+256])[:,16*h:16*h+WTOK] for h in range(HEADS)],axis=0).astype(BF16)
     dqT=jnp.concatenate([nn(kT[32*h:32*h+32],dsc[:,128*h:128*h+256])[:,16*h:16*h+WTOK] for h in range(HEADS)],axis=0).astype(BF16)
+    yield
     ctx=nt(eye144,ctxT).astype(BF16)
     dq=nt(eye144,dqT).astype(BF16)
+    yield
     dv=nn(ph,dblk).astype(BF16)
     dk=nn(dsc,qblk).astype(BF16)
     o_scr[0,toks]=(x+nn(ctx,wp)).astype(BF16)
+    yield
     ng=nt(dq,wq)+nt(dk,wk)+nt(dv,wv)
     g=ng*gain
     br=inv*(g-jnp.mean(g,axis=-1,keepdims=True)-std*jnp.mean(g*std,axis=-1,keepdims=True))
     o_scr[1,toks]=(u.astype(F32)+br).astype(BF16)
     rows=pl.ds(base+w*WTOK,WTOK)
     normed_scr[rows]=normed; gq_scr[rows]=dq; gk_scr[rows]=dk; gv_scr[rows]=dv; ctx_scr[rows]=ctx; up_scr[rows]=u
-    return jnp.sum(ng*std,axis=0,keepdims=True), jnp.sum(ng,axis=0,keepdims=True)
+    result.append((jnp.sum(ng*std,axis=0,keepdims=True), jnp.sum(ng,axis=0,keepdims=True)))
 
 def kernel(tl_ref,tr_ref,bl_ref,br_ref,left_ref,right_ref,perm_ref,back_ref,
            gain_ref,shift_ref,wq_ref,wk_ref,wv_ref,wkT_ref,wvT_ref,wp_ref,bias_ref,
            otl_ref,otr_ref,obl_ref,obr_ref,oleft_ref,oright_ref,fold_ref,wgrad_ref,x_scr,o_scr,*scr):
     w_scr,ngrad_scr=scr[13:]
     a=pl.program_id(0); pair=pl.program_id(1)
-    step=a*2+pair
+    step=a*(4//NW)+pair
     half=slice(0,WTOK); rest=slice(WTOK,2*WTOK)
     @pl.when((a==0)&(pair==0))
     def _():
@@ -154,29 +162,31 @@
             t=jnp.concatenate([left_ref[s,half],right_ref[s,half],left_ref[s,rest],right_ref[s,rest]],axis=0)
             x_scr[s]=nn(perm_ref[...],t).astype(BF16)
     eye=(lax.broadcasted_iota(jnp.int32,(WTOK,WTOK),0)==lax.broadcasted_iota(jnp.int32,(WTOK,WTOK),1)).astype(BF16)
-    base=pl.multiple_of(step*2*WTOK,2*WTOK)
+    base=pl.multiple_of(step*NW*WTOK,NW*WTOK)
     gs=[]
-    for w in range(2):
-        gs.append(window(w,pair*2+w,x_scr,o_scr,gain_ref[...],shift_ref[...],wq_ref[...],wk_ref[...],wv_ref[...],wkT_ref[...],wvT_ref[...],wp_ref[...],bias_ref,
-            fold_ref,*scr[:13],eye,base))
-    @pl.when((a==0)&(pair==1))
+    live=[window(w,pair*NW+w,x_scr,o_scr,gain_ref[...],shift_ref[...],wq_ref[...],wk_ref[...],wv_ref[...],wkT_ref[...],wvT_ref[...],wp_ref[...],bias_ref,
+            fold_ref,*scr[:13],eye,base,gs) for w in range(NW)]
+    done=object()
+    while live:
+        live=[g for g in live if next(g,done) is not done]
+    @pl.when((a==0)&(pair==4//NW-1))
     def _():
         for s in range(2):
             t=nn(back_ref[...],o_scr[s]).astype(BF16)
             for n,ref in enumerate((otl_ref,otr_ref,obl_ref,obr_ref)):
                 ref[s]=t[WTOK*n:WTOK*(n+1)]
-    @pl.when((a==1)&(pair==1))
+    @pl.when((a==1)&(pair==4//NW-1))
     def _():
         for s in range(2):
             t=nn(back_ref[...],o_scr[s]).astype(BF16)
             oleft_ref[s,half]=t[:WTOK]; oright_ref[s,half]=t[WTOK:2*WTOK]
             oleft_ref[s,rest]=t[2*WTOK:3*WTOK]; oright_ref[s,rest]=t[3*WTOK:]
-    both=jnp.concatenate([gs[0][0]+gs[1][0],gs[0][1]+gs[1][1],jnp.zeros((6,C),F32)],axis=0)
+    both=jnp.concatenate([sum(g[0] for g in gs),sum(g[1] for g in gs),jnp.zeros((6,C),F32)],axis=0)
     @pl.when(step==0)
     def _(): ngrad_scr[...]=both
     @pl.when(step>0)
     def _(): ngrad_scr[...]+=both
-    @pl.when(step==3)
+    @pl.when(step==8//NW-1)
     def _():
         normed_scr,gq_scr,gk_scr,gv_scr,ctx_scr,up_scr=scr[5:11]
         n=normed_scr[...]
@@ -209,16 +219,16 @@
     grids=[full(*p.shape) for p in parts]
     return pl.pallas_call(
         kernel,
-        grid=(2,2),
-        in_specs=grids+[full(4*WTOK,4*WTOK)]*2+[full(1,C),full(1,C)]+[full(C,C)]*6+[pl.BlockSpec((1,HEADS,2,WZ,WZ,24,128),lambda i,j:(i,0,j,0,0,0,0))],
-        out_specs=grids+[pl.BlockSpec((1,2,192,128),lambda i,j:(i,j,0,0)),full(2*64*16,128)],
+        grid=(2,4//NW),
+        in_specs=grids+[full(4*WTOK,4*WTOK)]*2+[full(1,C),full(1,C)]+[full(C,C)]*6+[pl.BlockSpec((1,HEADS,NW,WZ,WZ,24,128),lambda i,j:(i,0,j,0,0,0,0))],
+        out_specs=grids+[pl.BlockSpec((1,NW,192,128),lambda i,j:(i,j,0,0)),full(2*64*16,128)],
         out_shape=[jax.ShapeDtypeStruct(p.shape,BF16) for p in parts]+[
                    jax.ShapeDtypeStruct((2,4,192,128),F32),
                    jax.ShapeDtypeStruct((2*64*16,128),F32)],
         scratch_shapes=[pltpu.VMEM((2,4*WTOK,C),BF16),pltpu.VMEM((2,4*WTOK,C),BF16),
-                        pltpu.VMEM((2,WTOK,QP),F32),pltpu.VMEM((2,WTOK,QP),F32),pltpu.VMEM((2,WTOK,QP),BF16),pltpu.VMEM((2,WTOK,QP),BF16),
-                        pltpu.VMEM((2,HEADS,WZ,WZ,24,128),F32)]+[pltpu.VMEM((tok,C),BF16)]*6
-                       +[pltpu.VMEM((2,192,128),F32),pltpu.VMEM((2,24,128),F32)]+[pltpu.VMEM((6*C,128),F32),pltpu.VMEM((8,C),F32)],
+                        pltpu.VMEM((NW,WTOK,QP),F32),pltpu.VMEM((NW,WTOK,QP),F32),pltpu.VMEM((NW,WTOK,QP),BF16),pltpu.VMEM((NW,WTOK,QP),BF16),
+                        pltpu.VMEM((NW,HEADS,WZ,WZ,24,128),F32)]+[pltpu.VMEM((tok,C),BF16)]*6
+                       +[pltpu.VMEM((NW,192,128),F32),pltpu.VMEM((NW,24,128),F32)]+[pltpu.VMEM((6*C,128),F32),pltpu.VMEM((8,C),F32)],
         compiler_params=pltpu.CompilerParams(dimension_semantics=("arbitrary","arbitrary"),vmem_limit_bytes=32*1024*1024),
         cost_estimate=pl.CostEstimate(flops=6*10**9,bytes_accessed=8000000,transcendentals=10**6),
         name="attend",
@@ -299,48 +309,60 @@
     return lax.ppermute(block, LON + LAT, route)
 
 
-def pack_kernel(x_ref, u_ref, *outs):
-    west, east = slice(0, WLON // 2), slice(WLON // 2, WLON)
-    upper, middle, lower = slice(0, WLAT // 2), slice(WLAT // 2, 3 * WLAT // 2), slice(3 * WLAT // 2, 2 * WLAT)
-    places = ((middle, west), (upper, east), (lower, east), (lower, west), (upper, west), (middle, east))
-    for ref, (rows, cols) in zip(outs, places):
-        ref[0] = x_ref[rows, cols]
-        ref[1] = u_ref[rows, cols]
-
-
-def pack(x, u):
-    whole = pl.BlockSpec(memory_space=pltpu.VMEM)
-    half = WLON // 2
-    shapes = [(2, rows, half, 8, C) for rows in (6, 3, 3, 3, 3, 6)]
-    return pl.pallas_call(
-        pack_kernel,
-        in_specs=[whole, whole],
-        out_specs=[whole] * 6,
+def pack_kernel(places, x_ref, u_ref, *refs):
+    count = len(places)
+    outs, held, sems = refs[:count], refs[count : 2 * count], refs[-1]
+    arrive, leave = [], []
+    for n, (rows, cols) in enumerate(places):
+        for s, src in enumerate((x_ref, u_ref)):
+            arrive.append(pltpu.make_async_copy(src.at[rows, cols], held[n].at[s], sems.at[0, n, s]))
+            leave.append(pltpu.make_async_copy(held[n].at[s], outs[n].at[s], sems.at[1, n, s]))
+    for copy in arrive:
+        copy.start()
+    for first, second in zip(arrive, leave):
+        first.wait()
+        second.start()
+    for copy in leave:
+        copy.wait()
+
+
+def pack(x, u, places):
+    shapes = [(2, rows.size, cols.size, 8, C) for rows, cols in places]
+    outs = pl.pallas_call(
+        functools.partial(pack_kernel, places),
+        in_specs=[pl.BlockSpec(memory_space=pl.ANY)] * 2,
+        out_specs=[pl.BlockSpec(memory_space=pl.ANY)] * len(places),
         out_shape=[jax.ShapeDtypeStruct(s, BF16) for s in shapes],
-        compiler_params=pltpu.CompilerParams(vmem_limit_bytes=8 * 1024 * 1024),
+        scratch_shapes=[pltpu.VMEM(s, BF16) for s in shapes] + [pltpu.SemaphoreType.DMA((2, len(places), 2))],
+        compiler_params=pltpu.CompilerParams(vmem_limit_bytes=60 * 1024 * 1024),
         name="pack",
     )(x, u)
+    return [p.reshape(2, -1, C) for p in outs]
 
 
 def on_device(air_state, cotangent, norm_gain, norm_shift, qkv_weight, proj_weight, earth_bias):
     half = WLON // 2
-    sent_right, sent_bottom, sent_corner, sent_above, own_upper, own_middle = [
-        p.reshape(2, -1, C) for p in pack(air_state.transpose(1, 2, 0, 3), cotangent.transpose(1, 2, 0, 3))
-    ]
-    right = across(sent_right, -1, 0)
-    bottom = across(sent_bottom, 1, 0)
-    corner = across(sent_corner, 1, 1)
+    west, east = pl.ds(0, half), pl.ds(half, half)
+    upper, middle, lower = pl.ds(0, WLAT // 2), pl.ds(WLAT // 2, WLAT), pl.ds(3 * WLAT // 2, WLAT // 2)
+    x, u = air_state.transpose(1, 2, 0, 3), cotangent.transpose(1, 2, 0, 3)
+    sent_left, sent_corner, sent_above, sent_bottom = pack(
+        x, u, ((middle, east), (lower, west), (lower, east), (upper, west))
+    )
+    left = across(sent_left, 1, 0)
+    corner = across(sent_corner, -1, 1)
     above = across(sent_above, 0, 1)
-    parts = [corner, above, bottom, own_upper, own_middle, right]
+    bottom = across(sent_bottom, -1, 0)
+    own_upper, own_middle = pack(x, u, ((upper, east), (middle, west)))
+    parts = [above, corner, own_upper, bottom, left, own_middle]
     table = spread_table(earth_bias, lax.axis_index(LAT))
     *outs, fold, wgrad = attend(parts, norm_gain, norm_shift, qkv_weight, proj_weight, table)
     wgrad = wgrad.reshape(2, 64, 16, 128)[:, :, :11].astype(BF16)
 
-    corner, above, bottom, own_upper, own_middle, right = outs
-    right = across(right, 1, 0)
-    bottom = across(bottom, -1, 0)
-    corner = across(corner, -1, -1)
+    above, corner, own_upper, bottom, left, own_middle = outs
+    left = across(left, -1, 0)
+    corner = across(corner, 1, -1)
     above = across(above, 0, -1)
+    bottom = across(bottom, 1, 0)
 
     core = lax.axis_index("c")
     kept = lax.dynamic_index_in_dim(wgrad, core, 0, keepdims=False)
@@ -355,7 +377,7 @@
     bsum = jnp.pad(bsum, (0, 20 * 128 - bsum.shape[0])).reshape(20, 128)
     shard = jnp.concatenate((bsum, wsum), axis=0).astype(BF16)
     shard = jnp.pad(shard, ((0, 1), (0, 0)))
-    shard, right, bottom, corner, above = lax.optimization_barrier((shard, right, bottom, corner, above))
+    shard, left, bottom, corner, above = lax.optimization_barrier((shard, left, bottom, corner, above))
     spread = lax.all_to_all(jnp.broadcast_to(shard, (64,) + shard.shape), LON, 0, 0, tiled=True)
     bias_grad = spread[:, :20].reshape(64, 2560)[:, :2484].reshape(2, ZWIN, HEADS, POSITIONS)
     whalf = spread[:, 20:29]
@@ -372,7 +394,7 @@
     def joined(left, right):
         return jnp.concatenate([t.reshape(2, -1, half, 8, C) for t in (left, right)], axis=2)
 
-    grid = jnp.concatenate((joined(own_upper, bottom), joined(right, own_middle), joined(above, corner)), axis=1)
+    grid = jnp.concatenate((joined(bottom, own_upper), joined(own_middle, left), joined(corner, above)), axis=1)
     both = grid.transpose(0, 3, 1, 2, 4)
 
     return both[0], both[1], wall[:, : 3 * C], wall[:, 3 * C :], gain_grad, shift_grad, bias_grad

time: 110 us -> 103 us (0.936)
  waiting for transfers between devices: 38.1 us -> 32.6 us
  local copies, waits for them, and re-layouts: 10.6 us -> 7.82 us
  starting transfers between devices: 35.8 us -> 38.4 us
    ppermute x8, waiting for transfers between devices: 8.47 us -> 3.21 us  [across(): return lax.ppermute(block, LON + LAT, route)]
    unnamed x26 -> x22, local copies, waits for them, and re-layouts: 3.92 us -> 1.14 us
    all_to_all x1, starting transfers between devices: 4.63 us -> 6.93 us  [on_device(): parts = lax.all_to_all(payload, LON, 0, 0, tiled=True)]
    ppermute x4, starting transfers between devices: 3.64 us -> 4.88 us  [along(): lax.ppermute(block, axis, [(i, (i + distance) % size) for i in range(size)])]
    pallas_call x2 -> x3, Pallas kernels: 18.7 us -> 17.6 us  [the longest x1 13.7 us: attend(): pl.pallas_call(kernel, grid=(2, 4 // NW), in_specs=grids + [full(4 * WTOK...]
  transfers between devices with their start and end apart: 14 -> 14, of which waited for: 7 -> 5; matrix products, arithmetic and copies ran while one was open for 6% -> 6% of each run, Pallas kernels for 2% -> 4%
where the time goes in v1:
time: 103 us; the launch traced here: 102 us
  starting transfers between devices  38.4 us (37%)
  waiting for transfers between devices  32.6 us (32%)
  Pallas kernels  20.3 us (20%)
  local copies, waits for them, and re-layouts  7.82 us (8%)
  other arithmetic  2.25 us (2%)
    ppermute x8, starting transfers between devices, across(): return lax.ppermute(block, LON + LAT, route)  20.8 us
    all_to_all x1, waiting for transfers between devices, on_device(): lax.all_to_all(jnp.broadcast_to(shard, (64,) + shard.shape), LON, 0, 0, t...  16.9 us
    pallas_call x1, Pallas kernels, attend(): pl.pallas_call(kernel, grid=(2, 4 // NW), in_specs=grids + [full(4 * WTOK...  13.7 us
    all_to_all x1, waiting for transfers between devices, on_device(): parts = lax.all_to_all(payload, LON, 0, 0, tiled=True)  10.2 us
    all_to_all x1, starting transfers between devices, on_device(): parts = lax.all_to_all(payload, LON, 0, 0, tiled=True)  6.93 us
    all_to_all x1, starting transfers between devices, on_device(): lax.all_to_all(jnp.broadcast_to(shard, (64,) + shard.shape), LON, 0, 0, t...  5.78 us
    ppermute x4, starting transfers between devices, along(): lax.ppermute(block, axis, [(i, (i + distance) % size) for i in range(size)])  4.88 us
    pallas_call x2, Pallas kernels, pack(): pl.pallas_call(functools.partial(pack_kernel, places), in_specs=[pl.Block...  3.91 us
  transfers between devices with their start and end apart: 14, of which 5 were waited for; matrix products, arithmetic and copies ran while one was open for 6% of the time, Pallas kernels for 4%

profile of v1, /device:TPU:1, one launch (start us, length us, event | category | flops | bytes accessed | tf_op | source)
XLA Modules:
  0.0 102.4 jit_solution(940993090504998980)
XLA Ops:
  0.6 2.0 %pack.2 = (bf16[2,6,6,8,192]{4,3,2,1,0:T(8,128)(2,1)}, bf16[2,3,6,8,192]{4,3,2,1,0:T(8,128)(2,1)}, bf16[2,3,6,8,192]{4,3,2,1,0:T(8,128)(2,1)}, bf16[2,3,6,8,192]{4,3,2,1,0:T(8,128)(2,1)}) custom-call(bf16[12,12,8,192]{3,2,1,0:T(8,128)(2,1)} %bitcast.60, bf16[12,12,8,192]{3,2,1,0:T(8,128)(2,1)} %bitcast.62), custom_call_target="tpu_custom_call" | custom-call | tf_op jit(solution)/shard_map/pack/pallas_call | solution.py:331
  2.7 2.5 %collective-permute-start.3 = (bf16[2,288,192]{2,1,0:T(8,128)(2,1)}, bf16[2,288,192]{2,1,0:T(8,128)(2,1)S(1)}, u32[]{:S(2)}, u32[]{:S(2)}) collective-permute-start(bf16[2,288,192]{2,1,0:T(8,128)(2,1)} %bitcast.78), channel_id=1, source_target_pairs={{0,4},{1,5},{2,6},{3,7},{4,8},{5,9},{6,10},{7,11},{8,12},{9,13},{1... | collective-permute-start | bytes 663560 | tf_op jit(solution)/shard_map/ppermute | solution.py:309
  5.2 3.6 %collective-permute-start = (bf16[2,144,192]{2,1,0:T(8,128)(2,1)}, bf16[2,144,192]{2,1,0:T(8,128)(2,1)S(1)}, u32[]{:S(2)}, u32[]{:S(2)}) collective-permute-start(bf16[2,144,192]{2,1,0:T(8,128)(2,1)} %bitcast.81), channel_id=1, source_target_pairs={{0,1},{1,2},{2,3},{3,0},{4,5},{5,6},{6,7},{7,4},{8,9},{9,10},{10,1... | collective-permute-start | bytes 331784 | tf_op jit(solution)/shard_map/ppermute | solution.py:309
  8.8 5.7 %collective-permute-start.1 = (bf16[2,144,192]{2,1,0:T(8,128)(2,1)}, bf16[2,144,192]{2,1,0:T(8,128)(2,1)S(1)}, u32[]{:S(2)}, u32[]{:S(2)}) collective-permute-start(bf16[2,144,192]{2,1,0:T(8,128)(2,1)} %bitcast.80), channel_id=1, source_target_pairs={{0,253},{1,254},{2,255},{3,252},{4,1},{5,2},{6,3},{7,0},{8,5},{9,6... | collective-permute-start | bytes 331784 | tf_op jit(solution)/shard_map/ppermute | solution.py:309
  14.5 1.9 %collective-permute-start.2 = (bf16[2,144,192]{2,1,0:T(8,128)(2,1)}, bf16[2,144,192]{2,1,0:T(8,128)(2,1)S(1)}, u32[]{:S(2)}, u32[]{:S(2)}) collective-permute-start(bf16[2,144,192]{2,1,0:T(8,128)(2,1)} %bitcast.79), channel_id=1, source_target_pairs={{0,252},{1,253},{2,254},{3,255},{4,0},{5,1},{6,2},{7,3},{8,4},{9,5... | collective-permute-start | bytes 331784 | tf_op jit(solution)/shard_map/ppermute | solution.py:309
  16.5 1.9 %pack.3 = (bf16[2,3,6,8,192]{4,3,2,1,0:T(8,128)(2,1)}, bf16[2,6,6,8,192]{4,3,2,1,0:T(8,128)(2,1)}) custom-call(bf16[12,12,8,192]{3,2,1,0:T(8,128)(2,1)} %bitcast.61, bf16[12,12,8,192]{3,2,1,0:T(8,128)(2,1)} %bitcast.63), custom_call_target="tpu_custom_call" | custom-call | tf_op jit(solution)/shard_map/pack/pallas_call | solution.py:331
  18.4 1.3 %reshape.106.t_ref = f32[48,3312]{1,0:T(8,128)S(1)} reshape(f32[2,6,4,3312]{3,2,1,0:T(4,128)} %bitcast.69) | data formatting | bytes 1271808 | tf_op jit(solution)/shard_map/reshape | solution.py:273
  20.0 2.7 %table.1 = f32[4608,128]{1,0:T(8,128)S(1)} custom-call(s32[1]{0:T(128)} %bitcast.12.lat_ref, f32[48,3312]{1,0:T(8,128)S(1)} %reshape.106.t_ref, bf16[828,896]{1,0:T(8,128)(2,1)S(1)} %copy-done), custom_call_target="tpu_custom_call" | custom-call | flops 854654976 | bytes 5000000 | tf_op jit(solution)/shard_map/table/pallas_call | solution.py:275
  22.9 13.7 %attend.1 = (bf16[2,144,192]{2,1,0:T(8,128)(2,1)S(1)}, bf16[2,144,192]{2,1,0:T(8,128)(2,1)S(1)}, bf16[2,144,192]{2,1,0:T(8,128)(2,1)S(1)}, bf16[2,144,192]{2,1,0...) custom-call(bf16[2,144,192]{2,1,0:T(8,128)(2,1)S(1)} %collective-per, ...), custom_call_target="tpu_custom_call" | custom-call | flops 6000000000 | bytes 8000000 | tf_op jit(solution)/shard_map/attend/pallas_call | solution.py:220
  36.6 1.0 %collective-permute-start.4 = (bf16[64,11,128]{2,1,0:T(8,128)(2,1)S(1)}, bf16[64,11,128]{2,1,0:T(8,128)(2,1)S(1)}, u32[]{:S(2)}, u32[]{:S(2)}) collective-permute-start(bf16[64,11,128]{2,1,0:T(8,128)(2,1)S(1)} %dynamic-slice_bitcast_fusion), channel_id=1, source_target_pairs={{0,1},{1,0},{2,3},{3,2},{4,5},{5,4},{6,7},{7,6},{8,9},{9,8},{10,11... | collective-permute-start | bytes 540680 | tf_op jit(solution)/shard_map/ppermute | solution.py:299
  37.8 1.1 %collective-permute-done.4 = bf16[64,11,128]{2,1,0:T(8,128)(2,1)S(1)} collective-permute-done((bf16[64,11,128]{2,1,0:T(8,128)(2,1)S(1)}, bf16[64,11,128]{2,1,0:T(8,128)(2,1)S(1)}, u32[]{:S(2)}, u32[]{:S(2)}) %collective-permute-start.4) | collective-permute-done | bytes 180256 | tf_op jit(solution)/shard_map/ppermute | solution.py:299
  38.9 0.9 pad_maximum_fusion
  39.9 6.9 %all-to-all-start = ((bf16[64,32,128]{2,1,0:T(8,128)(2,1)}), bf16[64,32,128]{2,1,0:T(8,128)(2,1)S(1)}, u32[]{:S(2)}, u32[]{:S(2)}) async-start(bf16[64,32,128]{2,1,0:T(8,128)(2,1)} %pad_maximum_fusion), calls=%async_computation | async-start | bytes 1048576 | tf_op jit(solution)/shard_map/all_to_all | solution.py:372
  46.8 5.8 %collective-permute-start.6 = (bf16[2,288,192]{2,1,0:T(8,128)(2,1)S(1)}, bf16[2,288,192]{2,1,0:T(8,128)(2,1)S(1)}, u32[]{:S(2)}, u32[]{:S(2)}) collective-permute-start(bf16[2,288,192]{2,1,0:T(8,128)(2,1)S(1)} %get-tuple-element.34), channel_id=1, source_target_pairs={{0,252},{1,253},{2,254},{3,255},{4,0},{5,1},{6,2},{7,3},{8,4},{9,5... | collective-permute-start | bytes 663560 | tf_op jit(solution)/shard_map/ppermute | solution.py:309
  52.6 1.2 %collective-permute-start.9 = (bf16[2,144,192]{2,1,0:T(8,128)(2,1)S(1)}, bf16[2,144,192]{2,1,0:T(8,128)(2,1)S(1)}, u32[]{:S(2)}, u32[]{:S(2)}) collective-permute-start(bf16[2,144,192]{2,1,0:T(8,128)(2,1)S(1)} %get-tuple-element.37), channel_id=1, source_target_pairs={{0,3},{1,0},{2,1},{3,2},{4,7},{5,4},{6,5},{7,6},{8,11},{9,8},{10,9... | collective-permute-start | bytes 331784 | tf_op jit(solution)/shard_map/ppermute | solution.py:309
  53.8 10.2 %all-to-all-done = bf16[64,32,128]{2,1,0:T(8,128)(2,1)S(1)} async-done(((bf16[64,32,128]{2,1,0:T(8,128)(2,1)}), bf16[64,32,128]{2,1,0:T(8,128)(2,1)S(1)}, u32[]{:S(2)}, u32[]{:S(2)}) %all-to-all-start) | async-done | bytes 524320 | tf_op jit(solution)/shard_map/all_to_all | solution.py:372
  64.2 2.5 %collective-permute-start.5 = (f32[11,128]{1,0:T(8,128)S(1)}, f32[11,128]{1,0:T(8,128)S(1)}, u32[]{:S(2)}, u32[]{:S(2)}) collective-permute-start(f32[11,128]{1,0:T(8,128)S(1)} %slice.85), channel_id=1, source_target_pairs={{0,2},{2,0},{1,3},{3,1},{4,6},{6,4},{5,7},{7,5},{8,10},{10,8},{9,1... | collective-permute-start | bytes 16904 | tf_op jit(solution)/shard_map/ppermute | solution.py:299
  67.5 1.2 %collective-permute-done.5 = f32[11,128]{1,0:T(8,128)S(1)} collective-permute-done((f32[11,128]{1,0:T(8,128)S(1)}, f32[11,128]{1,0:T(8,128)S(1)}, u32[]{:S(2)}, u32[]{:S(2)}) %collective-permute-start.5) | collective-permute-done | bytes 5664 | tf_op jit(solution)/shard_map/ppermute | solution.py:299
  68.7 3.2 %collective-permute-done.8 = bf16[2,144,192]{2,1,0:T(8,128)(2,1)S(1)} collective-permute-done((bf16[2,144,192]{2,1,0:T(8,128)(2,1)S(1)}, bf16[2,144,192]{2,1,0:T(8,128)(2,1)S(1)}, u32[]{:S(2)}, u32[]{:S(2)}) %collective-permute-start.8) | collective-permute-done | bytes 110624 | tf_op jit(solution)/shard_map/ppermute | solution.py:309
  71.9 0.9 broadcast_in_dim.7
  72.8 5.8 %all-to-all-start.1 = ((bf16[64,32,128]{2,1,0:T(8,128)(2,1)}), bf16[64,32,128]{2,1,0:T(8,128)(2,1)S(1)}, u32[]{:S(2)}, u32[]{:S(2)}) async-start(bf16[64,32,128]{2,1,0:T(8,128)(2,1)} %broadcast_in_dim.7), calls=%async_computation.1 | async-start | bytes 1048576 | tf_op jit(solution)/shard_map/all_to_all | solution.py:381
  78.9 1.1 %slice_bitcast_fusion = (bf16[8,12,12,192]{3,0,2,1:T(8,128)(2,1)}, bf16[8,12,12,192]{3,0,2,1:T(8,128)(2,1)}) fusion(bf16[2,8,12,12,192]{4,1,3,2,0:T(8,128)(2,1)S(1)} %maximum_bitcast_fusion), kind=kLoop, calls=%fused_computation.2 | loop fusion | bytes 1769472 | tf_op jit(solution)/shard_map/squeeze | solution.py:400
  80.0 16.9 %all-to-all-done.1 = bf16[64,32,128]{2,1,0:T(8,128)(2,1)S(1)} async-done(((bf16[64,32,128]{2,1,0:T(8,128)(2,1)}), bf16[64,32,128]{2,1,0:T(8,128)(2,1)S(1)}, u32[]{:S(2)}, u32[]{:S(2)}) %all-to-all-start.1) | async-done | bytes 524320 | tf_op jit(solution)/shard_map/all_to_all | solution.py:381
  97.0 1.3 %collective-permute-start.10 = (bf16[64,9,128]{2,1,0:T(8,128)(2,1)S(1)}, bf16[64,9,128]{2,1,0:T(8,128)(2,1)S(1)}, u32[]{:S(2)}, u32[]{:S(2)}) collective-permute-start(bf16[64,9,128]{2,1,0:T(8,128)(2,1)S(1)} %slice.88), channel_id=1, source_target_pairs={{0,1},{1,0},{2,3},{3,2},{4,5},{5,4},{6,7},{7,6},{8,9},{9,8},{10,11... | collective-permute-start | bytes 442376 | tf_op jit(solution)/shard_map/ppermute | solution.py:299
  (63 shorter events, 6.0 us)
Async XLA Ops:
  0.6 15.8 %copy-start.8 = (bf16[192,576]{1,0:T(8,128)(2,1)S(1)}, bf16[192,576]{1,0:T(8,128)(2,1)}, u32[]{:S(2)}) copy-start(bf16[192,576]{1,0:T(8,128)(2,1)} %param.14) | copy-start | bytes 663556
  2.7 20.1 %collective-permute-start.3 = (bf16[2,288,192]{2,1,0:T(8,128)(2,1)}, bf16[2,288,192]{2,1,0:T(8,128)(2,1)S(1)}, u32[]{:S(2)}, u32[]{:S(2)}) collective-permute-start(bf16[2,288,192]{2,1,0:T(8,128)(2,1)} %bitcast.78), channel_id=1, source_target_pairs={{0,4},{1,5},{2,6},{3,7},{4,8},{5,9},{6,10},{7,11},{8,12},{9,13},{1... | collective-permute-start | bytes 663560 | tf_op jit(solution)/shard_map/ppermute | solution.py:309
  5.2 17.5 %collective-permute-start = (bf16[2,144,192]{2,1,0:T(8,128)(2,1)}, bf16[2,144,192]{2,1,0:T(8,128)(2,1)S(1)}, u32[]{:S(2)}, u32[]{:S(2)}) collective-permute-start(bf16[2,144,192]{2,1,0:T(8,128)(2,1)} %bitcast.81), channel_id=1, source_target_pairs={{0,1},{1,2},{2,3},{3,0},{4,5},{5,6},{6,7},{7,4},{8,9},{9,10},{10,1... | collective-permute-start | bytes 331784 | tf_op jit(solution)/shard_map/ppermute | solution.py:309
  8.8 14.0 %collective-permute-start.1 = (bf16[2,144,192]{2,1,0:T(8,128)(2,1)}, bf16[2,144,192]{2,1,0:T(8,128)(2,1)S(1)}, u32[]{:S(2)}, u32[]{:S(2)}) collective-permute-start(bf16[2,144,192]{2,1,0:T(8,128)(2,1)} %bitcast.80), channel_id=1, source_target_pairs={{0,253},{1,254},{2,255},{3,252},{4,1},{5,2},{6,3},{7,0},{8,5},{9,6... | collective-permute-start | bytes 331784 | tf_op jit(solution)/shard_map/ppermute | solution.py:309
  14.5 8.2 %collective-permute-start.2 = (bf16[2,144,192]{2,1,0:T(8,128)(2,1)}, bf16[2,144,192]{2,1,0:T(8,128)(2,1)S(1)}, u32[]{:S(2)}, u32[]{:S(2)}) collective-permute-start(bf16[2,144,192]{2,1,0:T(8,128)(2,1)} %bitcast.79), channel_id=1, source_target_pairs={{0,252},{1,253},{2,254},{3,255},{4,0},{5,1},{6,2},{7,3},{8,4},{9,5... | collective-permute-start | bytes 331784 | tf_op jit(solution)/shard_map/ppermute | solution.py:309
  16.5 3.4 %copy-start = (bf16[828,896]{1,0:T(8,128)(2,1)S(1)}, bf16[828,896]{1,0:T(8,128)(2,1)}, u32[]{:S(2)}) copy-start(bf16[828,896]{1,0:T(8,128)(2,1)} %constant.34.clone.hot_ref) | copy-start | bytes 4451332
  20.0 2.8 %copy-start.1 = (bf16[2,6,6,8,192]{4,3,2,1,0:T(8,128)(2,1)S(1)}, bf16[2,6,6,8,192]{4,3,2,1,0:T(8,128)(2,1)}, u32[]{:S(2)}) copy-start(bf16[2,6,6,8,192]{4,3,2,1,0:T(8,128)(2,1)} %get-tuple-element.31) | copy-start | bytes 663556
  20.0 2.8 %copy-start.2 = (bf16[2,3,6,8,192]{4,3,2,1,0:T(8,128)(2,1)S(1)}, bf16[2,3,6,8,192]{4,3,2,1,0:T(8,128)(2,1)}, u32[]{:S(2)}) copy-start(bf16[2,3,6,8,192]{4,3,2,1,0:T(8,128)(2,1)} %get-tuple-element.28) | copy-start | bytes 331780
  20.0 2.8 %copy-start.3 = (bf16[192,192]{1,0:T(8,128)(2,1)S(1)}, bf16[192,192]{1,0:T(8,128)(2,1)}, u32[]{:S(2)}) copy-start(bf16[192,192]{1,0:T(8,128)(2,1)} %wp_ref.1) | copy-start | bytes 221188
  20.0 2.8 %copy-start.4 = (f32[192]{0:T(256)S(1)}, f32[192]{0:T(256)}, u32[]{:S(2)}) copy-start(f32[192]{0:T(256)} %param.12) | copy-start | bytes 2308
  20.0 2.8 %copy-start.5 = (f32[192]{0:T(256)S(1)}, f32[192]{0:T(256)}, u32[]{:S(2)}) copy-start(f32[192]{0:T(256)} %param.13) | copy-start | bytes 2308
  20.0 2.8 %copy-start.6 = (bf16[576,576]{1,0:T(8,128)(2,1)S(1)}, bf16[576,576]{1,0:T(8,128)(2,1)}, u32[]{:S(2)}) copy-start(bf16[576,576]{1,0:T(8,128)(2,1)} %constant.35.clone.perm_ref) | copy-start | bytes 1990660
  20.0 2.8 %copy-start.7 = (bf16[576,576]{1,0:T(8,128)(2,1)S(1)}, bf16[576,576]{1,0:T(8,128)(2,1)}, u32[]{:S(2)}) copy-start(bf16[576,576]{1,0:T(8,128)(2,1)} %constant.36.clone.back_ref) | copy-start | bytes 1990660
  36.6 2.2 %collective-permute-start.4 = (bf16[64,11,128]{2,1,0:T(8,128)(2,1)S(1)}, bf16[64,11,128]{2,1,0:T(8,128)(2,1)S(1)}, u32[]{:S(2)}, u32[]{:S(2)}) collective-permute-start(bf16[64,11,128]{2,1,0:T(8,128)(2,1)S(1)} %dynamic-slice_bitcast_fusion), channel_id=1, source_target_pairs={{0,1},{1,0},{2,3},{3,2},{4,5},{5,4},{6,7},{7,6},{8,9},{9,8},{10,11... | collective-permute-start | bytes 540680 | tf_op jit(solution)/shard_map/ppermute | solution.py:299
  39.9 24.2 %all-to-all-start = ((bf16[64,32,128]{2,1,0:T(8,128)(2,1)}), bf16[64,32,128]{2,1,0:T(8,128)(2,1)S(1)}, u32[]{:S(2)}, u32[]{:S(2)}) async-start(bf16[64,32,128]{2,1,0:T(8,128)(2,1)} %pad_maximum_fusion), calls=%async_computation | async-start | bytes 1048576 | tf_op jit(solution)/shard_map/all_to_all | solution.py:372
  46.8 25.1 %collective-permute-start.6 = (bf16[2,288,192]{2,1,0:T(8,128)(2,1)S(1)}, bf16[2,288,192]{2,1,0:T(8,128)(2,1)S(1)}, u32[]{:S(2)}, u32[]{:S(2)}) collective-permute-start(bf16[2,288,192]{2,1,0:T(8,128)(2,1)S(1)} %get-tuple-element.34), channel_id=1, source_target_pairs={{0,252},{1,253},{2,254},{3,255},{4,0},{5,1},{6,2},{7,3},{8,4},{9,5... | collective-permute-start | bytes 663560 | tf_op jit(solution)/shard_map/ppermute | solution.py:309
  52.6 16.1 %collective-permute-start.7 = (bf16[2,144,192]{2,1,0:T(8,128)(2,1)S(1)}, bf16[2,144,192]{2,1,0:T(8,128)(2,1)S(1)}, u32[]{:S(2)}, u32[]{:S(2)}) collective-permute-start(bf16[2,144,192]{2,1,0:T(8,128)(2,1)S(1)} %get-tuple-element.35), channel_id=1, source_target_pairs={{0,4},{1,5},{2,6},{3,7},{4,8},{5,9},{6,10},{7,11},{8,12},{9,13},{1... | collective-permute-start | bytes 331784 | tf_op jit(solution)/shard_map/ppermute | solution.py:309
  52.6 19.3 %collective-permute-start.8 = (bf16[2,144,192]{2,1,0:T(8,128)(2,1)S(1)}, bf16[2,144,192]{2,1,0:T(8,128)(2,1)S(1)}, u32[]{:S(2)}, u32[]{:S(2)}) collective-permute-start(bf16[2,144,192]{2,1,0:T(8,128)(2,1)S(1)} %get-tuple-element.36), channel_id=1, source_target_pairs={{0,7},{1,4},{2,5},{3,6},{4,11},{5,8},{6,9},{7,10},{8,15},{9,12},{1... | collective-permute-start | bytes 331784 | tf_op jit(solution)/shard_map/ppermute | solution.py:309
  52.6 19.3 %collective-permute-start.9 = (bf16[2,144,192]{2,1,0:T(8,128)(2,1)S(1)}, bf16[2,144,192]{2,1,0:T(8,128)(2,1)S(1)}, u32[]{:S(2)}, u32[]{:S(2)}) collective-permute-start(bf16[2,144,192]{2,1,0:T(8,128)(2,1)S(1)} %get-tuple-element.37), channel_id=1, source_target_pairs={{0,3},{1,0},{2,1},{3,2},{4,7},{5,4},{6,5},{7,6},{8,11},{9,8},{10,9... | collective-permute-start | bytes 331784 | tf_op jit(solution)/shard_map/ppermute | solution.py:309
  64.2 4.5 %collective-permute-start.5 = (f32[11,128]{1,0:T(8,128)S(1)}, f32[11,128]{1,0:T(8,128)S(1)}, u32[]{:S(2)}, u32[]{:S(2)}) collective-permute-start(f32[11,128]{1,0:T(8,128)S(1)} %slice.85), channel_id=1, source_target_pairs={{0,2},{2,0},{1,3},{3,1},{4,6},{6,4},{5,7},{7,5},{8,10},{10,8},{9,1... | collective-permute-start | bytes 16904 | tf_op jit(solution)/shard_map/ppermute | solution.py:299
  72.8 24.1 %all-to-all-start.1 = ((bf16[64,32,128]{2,1,0:T(8,128)(2,1)}), bf16[64,32,128]{2,1,0:T(8,128)(2,1)S(1)}, u32[]{:S(2)}, u32[]{:S(2)}) async-start(bf16[64,32,128]{2,1,0:T(8,128)(2,1)} %broadcast_in_dim.7), calls=%async_computation.1 | async-start | bytes 1048576 | tf_op jit(solution)/shard_map/all_to_all | solution.py:381
  78.6 19.7 %collective-permute-start.11 = (f32[2,128]{1,0:T(2,128)S(1)}, f32[2,128]{1,0:T(2,128)S(1)}, u32[]{:S(2)}, u32[]{:S(2)}) collective-permute-start(f32[2,128]{1,0:T(2,128)S(1)} %slice.91), channel_id=1, source_target_pairs={{0,1},{1,0},{2,3},{3,2},{4,5},{5,4},{6,7},{7,6},{8,9},{9,8},{10,11... | collective-permute-start | bytes 3080 | tf_op jit(solution)/shard_map/ppermute | solution.py:299
  97.0 3.4 %collective-permute-start.10 = (bf16[64,9,128]{2,1,0:T(8,128)(2,1)S(1)}, bf16[64,9,128]{2,1,0:T(8,128)(2,1)S(1)}, u32[]{:S(2)}, u32[]{:S(2)}) collective-permute-start(bf16[64,9,128]{2,1,0:T(8,128)(2,1)S(1)} %slice.88), channel_id=1, source_target_pairs={{0,1},{1,0},{2,3},{3,2},{4,5},{5,4},{6,7},{7,6},{8,9},{9,8},{10,11... | collective-permute-start | bytes 442376 | tf_op jit(solution)/shard_map/ppermute | solution.py:299

commit v2 on v1

--- a/solution.py
+++ b/solution.py
@@ -33,7 +33,7 @@
 def window(w, b, x_scr,o_scr,gain,shift,wq,wk,wv,wkT,wvT,wp,bias_ref,
            fold_ref, s_scr,dp_scr,ph_scr,ds_scr,fold_scr, normed_scr,gq_scr,gk_scr,gv_scr,ctx_scr,up_scr,tail_scr,row7_scr,
            eye144, base, result):
-    toks=pl.ds(pl.multiple_of(b*WTOK,WTOK),WTOK)
+    toks=slice(b*WTOK,(b+1)*WTOK)
     x=x_scr[0,toks].astype(F32)
     u=x_scr[1,toks]
     mean=jnp.mean(x,axis=-1,keepdims=True)
@@ -140,67 +140,68 @@
     g=ng*gain
     br=inv*(g-jnp.mean(g,axis=-1,keepdims=True)-std*jnp.mean(g*std,axis=-1,keepdims=True))
     o_scr[1,toks]=(u.astype(F32)+br).astype(BF16)
-    rows=pl.ds(base+w*WTOK,WTOK)
+    rows=slice(base+w*WTOK,base+(w+1)*WTOK)
     normed_scr[rows]=normed; gq_scr[rows]=dq; gk_scr[rows]=dk; gv_scr[rows]=dv; ctx_scr[rows]=ctx; up_scr[rows]=u
     result.append((jnp.sum(ng*std,axis=0,keepdims=True), jnp.sum(ng,axis=0,keepdims=True)))
 
-def kernel(tl_ref,tr_ref,bl_ref,br_ref,left_ref,right_ref,perm_ref,back_ref,
-           gain_ref,shift_ref,wq_ref,wk_ref,wv_ref,wkT_ref,wvT_ref,wp_ref,bias_ref,
-           otl_ref,otr_ref,obl_ref,obr_ref,oleft_ref,oright_ref,fold_ref,wgrad_ref,x_scr,o_scr,*scr):
-    w_scr,ngrad_scr=scr[13:]
-    a=pl.program_id(0); pair=pl.program_id(1)
-    step=a*(4//NW)+pair
+def kernel(first, *refs):
+    count=2 if first else 4
+    ins=refs[:count]
+    perm_ref,back_ref,gain_ref,shift_ref,wqkv_ref,wp_ref,bias_ref=refs[count:count+7]
+    refs=refs[count+7:]
+    if first:
+        outs,refs=refs[:2],refs[2:]
+        fold_ref,w_ref,ngrad_ref,x_scr,o_scr=refs[:5]
+    else:
+        w_in,ngrad_in=refs[:2]
+        outs,refs=refs[2:6],refs[6:]
+        fold_ref,wgrad_ref,x_scr,o_scr,w_ref=refs[:5]
+    scr=refs[5:]
     half=slice(0,WTOK); rest=slice(WTOK,2*WTOK)
-    @pl.when((a==0)&(pair==0))
-    def _():
-        for s in range(2):
-            t=jnp.concatenate([tl_ref[s],tr_ref[s],bl_ref[s],br_ref[s]],axis=0)
-            x_scr[s]=nn(perm_ref[...],t).astype(BF16)
-    @pl.when((a==1)&(pair==0))
-    def _():
-        for s in range(2):
-            t=jnp.concatenate([left_ref[s,half],right_ref[s,half],left_ref[s,rest],right_ref[s,rest]],axis=0)
-            x_scr[s]=nn(perm_ref[...],t).astype(BF16)
+    for s in range(2):
+        if first:
+            t=[ins[0][s,half],ins[1][s,half],ins[0][s,rest],ins[1][s,rest]]
+        else:
+            t=[ref[s] for ref in ins]
+        x_scr[s]=nn(perm_ref[...],jnp.concatenate(t,axis=0)).astype(BF16)
     eye=(lax.broadcasted_iota(jnp.int32,(WTOK,WTOK),0)==lax.broadcasted_iota(jnp.int32,(WTOK,WTOK),1)).astype(BF16)
-    base=pl.multiple_of(step*NW*WTOK,NW*WTOK)
+    wqkv=wqkv_ref[...]
+    wq,wk,wv=wqkv[:,:C],wqkv[:,C:2*C],wqkv[:,2*C:]
+    flip=(lax.broadcasted_iota(jnp.int32,(C,C),0)==lax.broadcasted_iota(jnp.int32,(C,C),1)).astype(BF16)
+    wkT,wvT=nt(flip,wk).astype(BF16),nt(flip,wv).astype(BF16)
     gs=[]
-    live=[window(w,pair*NW+w,x_scr,o_scr,gain_ref[...],shift_ref[...],wq_ref[...],wk_ref[...],wv_ref[...],wkT_ref[...],wvT_ref[...],wp_ref[...],bias_ref,
-            fold_ref,*scr[:13],eye,base,gs) for w in range(NW)]
+    live=[window(w,w,x_scr,o_scr,gain_ref[...],shift_ref[...],wq,wk,wv,wkT,wvT,wp_ref[...],bias_ref,
+            fold_ref,*scr,eye,0,gs) for w in range(NW)]
     done=object()
     while live:
         live=[g for g in live if next(g,done) is not done]
-    @pl.when((a==0)&(pair==4//NW-1))
-    def _():
-        for s in range(2):
-            t=nn(back_ref[...],o_scr[s]).astype(BF16)
-            for n,ref in enumerate((otl_ref,otr_ref,obl_ref,obr_ref)):
+    for s in range(2):
+        t=nn(back_ref[...],o_scr[s]).astype(BF16)
+        if first:
+            outs[0][s,half]=t[:WTOK]; outs[1][s,half]=t[WTOK:2*WTOK]
+            outs[0][s,rest]=t[2*WTOK:3*WTOK]; outs[1][s,rest]=t[3*WTOK:]
+        else:
+            for n,ref in enumerate(outs):
                 ref[s]=t[WTOK*n:WTOK*(n+1)]
-    @pl.when((a==1)&(pair==4//NW-1))
-    def _():
-        for s in range(2):
-            t=nn(back_ref[...],o_scr[s]).astype(BF16)
-            oleft_ref[s,half]=t[:WTOK]; oright_ref[s,half]=t[WTOK:2*WTOK]
-            oleft_ref[s,rest]=t[2*WTOK:3*WTOK]; oright_ref[s,rest]=t[3*WTOK:]
-    both=jnp.concatenate([sum(g[0] for g in gs),sum(g[1] for g in gs),jnp.zeros((6,C),F32)],axis=0)
-    @pl.when(step==0)
-    def _(): ngrad_scr[...]=both
-    @pl.when(step>0)
-    def _(): ngrad_scr[...]+=both
-    @pl.when(step==8//NW-1)
-    def _():
-        normed_scr,gq_scr,gk_scr,gv_scr,ctx_scr,up_scr=scr[5:11]
-        n=normed_scr[...]
-        whole=jnp.concatenate([tn(n,gq_scr[...]),tn(n,gk_scr[...]),tn(n,gv_scr[...]),tn(ctx_scr[...],up_scr[...])],axis=1)
+    normed_scr,gq_scr,gk_scr,gv_scr,ctx_scr,up_scr=scr[5:11]
+    n=normed_scr[...]
+    whole=jnp.concatenate([tn(n,gq_scr[...]),tn(n,gk_scr[...]),tn(n,gv_scr[...]),tn(ctx_scr[...],up_scr[...])],axis=1)
+    ng=jnp.concatenate([sum(g[0] for g in gs),sum(g[1] for g in gs),jnp.zeros((6,C),F32)],axis=0)
+    if first:
         for t in range(6):
-            w_scr[C*t:C*(t+1)]=whole[:,128*t:128*(t+1)]
-        for r in range(3):
-            for t in range(6):
-                m=r*6+t
-                wgrad_ref[pl.ds((m//9)*64*16+m%9,64,stride=16),:]=w_scr[pl.ds(C*t+r,64,stride=3),:]
-        ng=ngrad_scr[...]
-        for half in range(2):
-            wgrad_ref[pl.ds(half*64*16+9,64,stride=16),:]=jnp.broadcast_to(ng[half:half+1,:128],(64,128))
-            wgrad_ref[pl.ds(half*64*16+10,64,stride=16),:]=jnp.broadcast_to(jnp.concatenate([ng[half:half+1,128:],jnp.zeros((1,64),F32)],axis=1),(64,128))
+            w_ref[C*t:C*(t+1)]=whole[:,128*t:128*(t+1)]
+        ngrad_ref[...]=ng
+        return
+    for t in range(6):
+        w_ref[C*t:C*(t+1)]=whole[:,128*t:128*(t+1)]+w_in[C*t:C*(t+1)]
+    ng=ng+ngrad_in[...]
+    for r in range(3):
+        for t in range(6):
+            m=r*6+t
+            wgrad_ref[pl.ds((m//9)*64*16+m%9,64,stride=16),:]=w_ref[pl.ds(C*t+r,64,stride=3),:]
+    for h in range(2):
+        wgrad_ref[pl.ds(h*64*16+9,64,stride=16),:]=jnp.broadcast_to(ng[h:h+1,:128],(64,128))
+        wgrad_ref[pl.ds(h*64*16+10,64,stride=16),:]=jnp.broadcast_to(jnp.concatenate([ng[h:h+1,128:],jnp.zeros((1,64),F32)],axis=1),(64,128))
 
 def token_order():
     hot=np.zeros((576,576),np.float32)
@@ -211,28 +212,30 @@
                 hot[(lev*WLON+w)*WLAT+h,quad*WTOK+h%3*48+w%6*8+(lev-1)%8]=1.0
     return hot
 
-def attend(parts,gain,shift,wqkv,wp,vtab):
-    wq,wk,wv=wqkv[:,:C],wqkv[:,C:2*C],wqkv[:,2*C:]
-    full=lambda *s: pl.BlockSpec(s,lambda i,j:(0,)*len(s))
-    tok=8*WTOK
+def attend(row,parts,weights,vtab,sums=()):
+    first=row==1
+    full=lambda *s: pl.BlockSpec(s,lambda i:(0,)*len(s))
+    tok=4*WTOK
     hot=token_order()
-    grids=[full(*p.shape) for p in parts]
+    own=[full(*p.shape) for p in parts]
+    wsum=pltpu.VMEM((6*C,128),F32)
+    ends=[(6*C,128),(8,C)] if first else [(2*64*16,128)]
     return pl.pallas_call(
-        kernel,
-        grid=(2,4//NW),
-        in_specs=grids+[full(4*WTOK,4*WTOK)]*2+[full(1,C),full(1,C)]+[full(C,C)]*6+[pl.BlockSpec((1,HEADS,NW,WZ,WZ,24,128),lambda i,j:(i,0,j,0,0,0,0))],
-        out_specs=grids+[pl.BlockSpec((1,NW,192,128),lambda i,j:(i,j,0,0)),full(2*64*16,128)],
-        out_shape=[jax.ShapeDtypeStruct(p.shape,BF16) for p in parts]+[
-                   jax.ShapeDtypeStruct((2,4,192,128),F32),
-                   jax.ShapeDtypeStruct((2*64*16,128),F32)],
-        scratch_shapes=[pltpu.VMEM((2,4*WTOK,C),BF16),pltpu.VMEM((2,4*WTOK,C),BF16),
-                        pltpu.VMEM((NW,WTOK,QP),F32),pltpu.VMEM((NW,WTOK,QP),F32),pltpu.VMEM((NW,WTOK,QP),BF16),pltpu.VMEM((NW,WTOK,QP),BF16),
+        functools.partial(kernel,first),
+        grid=(1,),
+        in_specs=own+[full(tok,tok)]*2+[full(1,C),full(1,C),full(C,3*C),full(C,C)]
+                 +[pl.BlockSpec((1,HEADS,4,WZ,WZ,24,128),lambda i:(row,0,0,0,0,0,0))]+[full(*s.shape) for s in sums],
+        out_specs=own+[full(1,4,192,128)]+[full(*s) for s in ends],
+        out_shape=[jax.ShapeDtypeStruct(p.shape,BF16) for p in parts]+[jax.ShapeDtypeStruct((1,4,192,128),F32)]
+                  +[jax.ShapeDtypeStruct(s,F32) for s in ends],
+        scratch_shapes=[pltpu.VMEM((2,tok,C),BF16),pltpu.VMEM((2,tok,C),BF16)]+([] if first else [wsum])
+                       +[pltpu.VMEM((NW,WTOK,QP),F32),pltpu.VMEM((NW,WTOK,QP),F32),pltpu.VMEM((NW,WTOK,QP),BF16),pltpu.VMEM((NW,WTOK,QP),BF16),
                         pltpu.VMEM((NW,HEADS,WZ,WZ,24,128),F32)]+[pltpu.VMEM((tok,C),BF16)]*6
-                       +[pltpu.VMEM((NW,192,128),F32),pltpu.VMEM((NW,24,128),F32)]+[pltpu.VMEM((6*C,128),F32),pltpu.VMEM((8,C),F32)],
-        compiler_params=pltpu.CompilerParams(dimension_semantics=("arbitrary","arbitrary"),vmem_limit_bytes=32*1024*1024),
-        cost_estimate=pl.CostEstimate(flops=6*10**9,bytes_accessed=8000000,transcendentals=10**6),
-        name="attend",
-    )(*parts,jnp.asarray(hot,BF16),jnp.asarray(hot.T,BF16),gain.reshape(1,C),shift.reshape(1,C),wq,wk,wv,wk.T,wv.T,wp,vtab)
+                       +[pltpu.VMEM((NW,192,128),F32),pltpu.VMEM((NW,24,128),F32)],
+        compiler_params=pltpu.CompilerParams(dimension_semantics=("arbitrary",),vmem_limit_bytes=32*1024*1024),
+        cost_estimate=pl.CostEstimate(flops=3*10**9,bytes_accessed=4000000,transcendentals=5*10**5),
+        name="attend_first" if first else "attend_last",
+    )(*parts,jnp.asarray(hot,BF16),jnp.asarray(hot.T,BF16),*weights,vtab,*sums)
 
 def table_order():
     hot=np.zeros((828,896),np.float32)
@@ -252,7 +255,7 @@
     bottom=row%4==0
     hot=hot_ref[...]
     for zz in range(4):
-        t=t_ref[:,828*zz:828*(zz+1)]
+        t=jnp.concatenate([t_ref[a,h,:,828*zz:828*(zz+1)] for a in range(2) for h in range(HEADS)],axis=0)
         hi=t.astype(BF16); rest=t-hi.astype(F32)
         mid=rest.astype(BF16); lo=(rest-mid.astype(F32)).astype(BF16)
         v=nn(jnp.concatenate([hi,mid,lo],axis=0),hot)
@@ -270,7 +273,7 @@
                 out_ref[pl.ds(zz*24+dw*WLAT+hk,rows,stride=96),:]=jnp.where(cut,MASKED,r)
 
 def spread_table(earth_bias, lat):
-    flat=earth_bias.transpose(0,2,1,3).reshape(48,POSITIONS)
+    flat=earth_bias.transpose(0,2,1,3)
     whole=pl.BlockSpec(memory_space=pltpu.VMEM)
     out=pl.pallas_call(
         table_kernel,
@@ -345,21 +348,21 @@
     west, east = pl.ds(0, half), pl.ds(half, half)
     upper, middle, lower = pl.ds(0, WLAT // 2), pl.ds(WLAT // 2, WLAT), pl.ds(3 * WLAT // 2, WLAT // 2)
     x, u = air_state.transpose(1, 2, 0, 3), cotangent.transpose(1, 2, 0, 3)
-    sent_left, sent_corner, sent_above, sent_bottom = pack(
-        x, u, ((middle, east), (lower, west), (lower, east), (upper, west))
+    sent_left, sent_corner, sent_above, sent_bottom, own_upper, own_middle = pack(
+        x, u, ((middle, east), (lower, west), (lower, east), (upper, west), (upper, east), (middle, west))
     )
     left = across(sent_left, 1, 0)
     corner = across(sent_corner, -1, 1)
     above = across(sent_above, 0, 1)
     bottom = across(sent_bottom, -1, 0)
-    own_upper, own_middle = pack(x, u, ((upper, east), (middle, west)))
-    parts = [above, corner, own_upper, bottom, left, own_middle]
     table = spread_table(earth_bias, lax.axis_index(LAT))
-    *outs, fold, wgrad = attend(parts, norm_gain, norm_shift, qkv_weight, proj_weight, table)
+    weights = (norm_gain.reshape(1, C), norm_shift.reshape(1, C), qkv_weight, proj_weight)
+    left, own_middle, fold_first, *sums = attend(1, [left, own_middle], weights, table)
+    left = across(left, -1, 0)
+    above, corner, own_upper, bottom, fold_last, wgrad = attend(0, [above, corner, own_upper, bottom], weights, table, sums)
+    fold = jnp.concatenate((fold_last, fold_first))
     wgrad = wgrad.reshape(2, 64, 16, 128)[:, :, :11].astype(BF16)
 
-    above, corner, own_upper, bottom, left, own_middle = outs
-    left = across(left, -1, 0)
     corner = across(corner, 1, -1)
     above = across(above, 0, -1)
     bottom = across(bottom, 1, 0)

time: 103 us -> 99 us (0.961)
  Pallas kernels: 20.3 us -> 18.2 us
    all_to_all x1, starting transfers between devices: 6.93 us -> 4.79 us  [on_device(): parts = lax.all_to_all(payload, LON, 0, 0, tiled=True)]
    pallas_call x2 -> x1, Pallas kernels: 3.91 us -> 2.27 us  [pack(): pl.pallas_call(functools.partial(pack_kernel, places), in_specs=[pl.Block...]
    reshape x1 -> x0, local copies, waits for them, and re-layouts: 1.3 us -> none  [spread_table(): flat = earth_bias.transpose(0, 2, 1, 3).reshape(48, POSITIONS)]
    unnamed x22, local copies, waits for them, and re-layouts: 1.14 us -> 2.31 us
    pallas_call x1 -> x2, Pallas kernels: 13.7 us -> 13.2 us  [attend(): pl.pallas_call(functools.partial(kernel, first), grid=(1,), in_specs=own...]
  transfers between devices with their start and end apart: 14 -> 14, of which waited for: 5 -> 6; matrix products, arithmetic and copies ran while one was open for 6% -> 5% of each run, Pallas kernels for 4% -> 9%
where the time goes in v2:
time: 99 us; the launch traced here: 98.7 us
  starting transfers between devices  37.4 us (38%)
  waiting for transfers between devices  32.3 us (33%)
  Pallas kernels  18.2 us (18%)
  local copies, waits for them, and re-layouts  7.59 us (8%)
  other arithmetic  2.29 us (2%)
    ppermute x8, starting transfers between devices, across(): return lax.ppermute(block, LON + LAT, route)  21.6 us
    all_to_all x1, waiting for transfers between devices, on_device(): lax.all_to_all(jnp.broadcast_to(shard, (64,) + shard.shape), LON, 0, 0, t...  16.9 us
    pallas_call x2, Pallas kernels, attend(): pl.pallas_call(functools.partial(kernel, first), grid=(1,), in_specs=own...  13.2 us
    all_to_all x1, waiting for transfers between devices, on_device(): parts = lax.all_to_all(payload, LON, 0, 0, tiled=True)  9.41 us
    all_to_all x1, starting transfers between devices, on_device(): lax.all_to_all(jnp.broadcast_to(shard, (64,) + shard.shape), LON, 0, 0, t...  5.78 us
    ppermute x4, starting transfers between devices, along(): lax.ppermute(block, axis, [(i, (i + distance) % size) for i in range(size)])  5.26 us
    all_to_all x1, starting transfers between devices, on_device(): parts = lax.all_to_all(payload, LON, 0, 0, tiled=True)  4.79 us
    ppermute x8, waiting for transfers between devices, across(): return lax.ppermute(block, LON + LAT, route)  3.76 us
  transfers between devices with their start and end apart: 14, of which 6 were waited for; matrix products, arithmetic and copies ran while one was open for 5% of the time, Pallas kernels for 9%

profile of v2, /device:TPU:1, one launch (start us, length us, event | category | flops | bytes accessed | tf_op | source)
XLA Modules:
  0.0 98.7 jit_solution(13164172803194712011)
XLA Ops:
  0.6 2.3 %pack.1 = (bf16[2,6,6,8,192]{4,3,2,1,0:T(8,128)(2,1)}, bf16[2,3,6,8,192]{4,3,2,1,0:T(8,128)(2,1)}, bf16[2,3,6,8,192]{4,3,2,1,0:T(8,128)(2,1)}, bf16[2,3,6,8,192]...) custom-call(bf16[12,12,8,192]{3,2,1,0:T(8,128)(2,1)} %bitcast.65, ...), custom_call_target="tpu_custom_call" | custom-call | tf_op jit(solution)/shard_map/pack/pallas_call | solution.py:334
  2.9 2.5 %collective-permute-start.3 = (bf16[2,288,192]{2,1,0:T(8,128)(2,1)}, bf16[2,288,192]{2,1,0:T(8,128)(2,1)S(1)}, u32[]{:S(2)}, u32[]{:S(2)}) collective-permute-start(bf16[2,288,192]{2,1,0:T(8,128)(2,1)} %bitcast.75), channel_id=1, source_target_pairs={{0,4},{1,5},{2,6},{3,7},{4,8},{5,9},{6,10},{7,11},{8,12},{9,13},{1... | collective-permute-start | bytes 663560 | tf_op jit(solution)/shard_map/ppermute | solution.py:312
  5.5 3.6 %collective-permute-start = (bf16[2,144,192]{2,1,0:T(8,128)(2,1)}, bf16[2,144,192]{2,1,0:T(8,128)(2,1)S(1)}, u32[]{:S(2)}, u32[]{:S(2)}) collective-permute-start(bf16[2,144,192]{2,1,0:T(8,128)(2,1)} %bitcast.78), channel_id=1, source_target_pairs={{0,1},{1,2},{2,3},{3,0},{4,5},{5,6},{6,7},{7,4},{8,9},{9,10},{10,1... | collective-permute-start | bytes 331784 | tf_op jit(solution)/shard_map/ppermute | solution.py:312
  9.0 5.7 %collective-permute-start.1 = (bf16[2,144,192]{2,1,0:T(8,128)(2,1)}, bf16[2,144,192]{2,1,0:T(8,128)(2,1)S(1)}, u32[]{:S(2)}, u32[]{:S(2)}) collective-permute-start(bf16[2,144,192]{2,1,0:T(8,128)(2,1)} %bitcast.77), channel_id=1, source_target_pairs={{0,253},{1,254},{2,255},{3,252},{4,1},{5,2},{6,3},{7,0},{8,5},{9,6... | collective-permute-start | bytes 331784 | tf_op jit(solution)/shard_map/ppermute | solution.py:312
  14.8 1.9 %collective-permute-start.2 = (bf16[2,144,192]{2,1,0:T(8,128)(2,1)}, bf16[2,144,192]{2,1,0:T(8,128)(2,1)S(1)}, u32[]{:S(2)}, u32[]{:S(2)}) collective-permute-start(bf16[2,144,192]{2,1,0:T(8,128)(2,1)} %bitcast.76), channel_id=1, source_target_pairs={{0,252},{1,253},{2,254},{3,255},{4,0},{5,1},{6,2},{7,3},{8,4},{9,5... | collective-permute-start | bytes 331784 | tf_op jit(solution)/shard_map/ppermute | solution.py:312
  16.7 1.4 %copy-done = bf16[828,896]{1,0:T(8,128)(2,1)S(1)} copy-done((bf16[828,896]{1,0:T(8,128)(2,1)S(1)}, bf16[828,896]{1,0:T(8,128)(2,1)}, u32[]{:S(2)}) %copy-start) | copy-done | bytes 1483800
  18.1 2.8 %table.1 = f32[4608,128]{1,0:T(8,128)S(1)} custom-call(s32[1]{0:T(128)} %bitcast.8.lat_ref, f32[2,6,4,3312]{3,2,1,0:T(4,128)S(1)} %bitcast.51, bf16[828,896]{1,0:T(8,128)(2,1)S(1)} %copy-done), custom_call_target="tpu_custom_call" | custom-call | flops 854654976 | bytes 5000000 | tf_op jit(solution)/shard_map/table/pallas_call | solution.py:278
  21.4 6.3 %attend_first.1 = (bf16[2,288,192]{2,1,0:T(8,128)(2,1)S(1)}, bf16[2,288,192]{2,1,0:T(8,128)(2,1)S(1)}, f32[1,4,192,128]{3,2,1,0:T(8,128)S(1)}, f32[1152,128]{1,0:T(8,128)S(1)}, f32[8,192]{1,0:T(8,128)S(1)}) custom-call(bf16[2,288,192]{2,1,0:T(8,128)(2,1)S(1)} %collective-permute-done.3.refs_0_, bf16[2,288,192]{2,1,0:T(8,128)(2,1)S(1)} %bitcast.54, ...), custom_call_target="tpu_custom_call" | custom-call | flops 3000000000 | bytes 4000000 | tf_op jit(solution)/shard_map/attend_first/pallas_call | solution.py:223
  27.8 6.9 %attend_last.1 = (bf16[2,144,192]{2,1,0:T(8,128)(2,1)S(1)}, bf16[2,144,192]{2,1,0:T(8,128)(2,1)S(1)}, bf16[2,144,192]{2,1,0:T(8,128)(2,1)S(1)}, bf16[2,144,192]{...) custom-call(bf16[2,144,192]{2,1,0:T(8,128)(2,1)S(1)} %collective-permute-done.refs_0_, ...), custom_call_target="tpu_custom_call" | custom-call | flops 3000000000 | bytes 4000000 | tf_op jit(solution)/shard_map/attend_last/pallas_call | solution.py:223
  34.7 1.4 %collective-permute-start.4 = (bf16[64,11,128]{2,1,0:T(8,128)(2,1)S(1)}, bf16[64,11,128]{2,1,0:T(8,128)(2,1)S(1)}, u32[]{:S(2)}, u32[]{:S(2)}) collective-permute-start(bf16[64,11,128]{2,1,0:T(8,128)(2,1)S(1)} %dynamic-slice_bitcast_fusion), channel_id=1, source_target_pairs={{0,1},{1,0},{2,3},{3,2},{4,5},{5,4},{6,7},{7,6},{8,9},{9,8},{10,11... | collective-permute-start | bytes 540680 | tf_op jit(solution)/shard_map/ppermute | solution.py:302
  36.2 1.0 %collective-permute-done.4 = bf16[64,11,128]{2,1,0:T(8,128)(2,1)S(1)} collective-permute-done((bf16[64,11,128]{2,1,0:T(8,128)(2,1)S(1)}, bf16[64,11,128]{2,1,0:T(8,128)(2,1)S(1)}, u32[]{:S(2)}, u32[]{:S(2)}) %collective-permute-start.4) | collective-permute-done | bytes 180256 | tf_op jit(solution)/shard_map/ppermute | solution.py:302
  38.3 4.8 %all-to-all-start = ((bf16[64,32,128]{2,1,0:T(8,128)(2,1)}), bf16[64,32,128]{2,1,0:T(8,128)(2,1)S(1)}, u32[]{:S(2)}, u32[]{:S(2)}) async-start(bf16[64,32,128]{2,1,0:T(8,128)(2,1)} %pad_maximum_fusion), calls=%async_computation | async-start | bytes 1048576 | tf_op jit(solution)/shard_map/all_to_all | solution.py:375
  43.1 1.1 %collective-permute-start.7 = (bf16[2,144,192]{2,1,0:T(8,128)(2,1)S(1)}, bf16[2,144,192]{2,1,0:T(8,128)(2,1)S(1)}, u32[]{:S(2)}, u32[]{:S(2)}) collective-permute-start(bf16[2,144,192]{2,1,0:T(8,128)(2,1)S(1)} %get-tuple-element.41), channel_id=1, source_target_pairs={{0,4},{1,5},{2,6},{3,7},{4,8},{5,9},{6,10},{7,11},{8,12},{9,13},{1... | collective-permute-start | bytes 331784 | tf_op jit(solution)/shard_map/ppermute | solution.py:312
  44.2 2.3 %collective-permute-start.8 = (bf16[2,144,192]{2,1,0:T(8,128)(2,1)S(1)}, bf16[2,144,192]{2,1,0:T(8,128)(2,1)S(1)}, u32[]{:S(2)}, u32[]{:S(2)}) collective-permute-start(bf16[2,144,192]{2,1,0:T(8,128)(2,1)S(1)} %get-tuple-element.42), channel_id=1, source_target_pairs={{0,7},{1,4},{2,5},{3,6},{4,11},{5,8},{6,9},{7,10},{8,15},{9,12},{1... | collective-permute-start | bytes 331784 | tf_op jit(solution)/shard_map/ppermute | solution.py:312
  46.4 1.5 %collective-permute-start.9 = (bf16[2,144,192]{2,1,0:T(8,128)(2,1)S(1)}, bf16[2,144,192]{2,1,0:T(8,128)(2,1)S(1)}, u32[]{:S(2)}, u32[]{:S(2)}) collective-permute-start(bf16[2,144,192]{2,1,0:T(8,128)(2,1)S(1)} %get-tuple-element.43), channel_id=1, source_target_pairs={{0,3},{1,0},{2,1},{3,2},{4,7},{5,4},{6,5},{7,6},{8,11},{9,8},{10,9... | collective-permute-start | bytes 331784 | tf_op jit(solution)/shard_map/ppermute | solution.py:312
  47.9 3.0 %collective-permute-start.6 = (bf16[2,288,192]{2,1,0:T(8,128)(2,1)S(1)}, bf16[2,288,192]{2,1,0:T(8,128)(2,1)S(1)}, u32[]{:S(2)}, u32[]{:S(2)}) collective-permute-start(bf16[2,288,192]{2,1,0:T(8,128)(2,1)S(1)} %get-tuple-element.40), channel_id=1, source_target_pairs={{0,252},{1,253},{2,254},{3,255},{4,0},{5,1},{6,2},{7,3},{8,4},{9,5... | collective-permute-start | bytes 663560 | tf_op jit(solution)/shard_map/ppermute | solution.py:312
  50.9 9.4 %all-to-all-done = bf16[64,32,128]{2,1,0:T(8,128)(2,1)S(1)} async-done(((bf16[64,32,128]{2,1,0:T(8,128)(2,1)}), bf16[64,32,128]{2,1,0:T(8,128)(2,1)S(1)}, u32[]{:S(2)}, u32[]{:S(2)}) %all-to-all-start) | async-done | bytes 524320 | tf_op jit(solution)/shard_map/all_to_all | solution.py:375
  60.5 2.5 %collective-permute-start.5 = (f32[11,128]{1,0:T(8,128)S(1)}, f32[11,128]{1,0:T(8,128)S(1)}, u32[]{:S(2)}, u32[]{:S(2)}) collective-permute-start(f32[11,128]{1,0:T(8,128)S(1)} %slice.73), channel_id=1, source_target_pairs={{0,2},{2,0},{1,3},{3,1},{4,6},{6,4},{5,7},{7,5},{8,10},{10,8},{9,1... | collective-permute-start | bytes 16904 | tf_op jit(solution)/shard_map/ppermute | solution.py:302
  63.8 1.2 %collective-permute-done.5 = f32[11,128]{1,0:T(8,128)S(1)} collective-permute-done((f32[11,128]{1,0:T(8,128)S(1)}, f32[11,128]{1,0:T(8,128)S(1)}, u32[]{:S(2)}, u32[]{:S(2)}) %collective-permute-start.5) | collective-permute-done | bytes 5664 | tf_op jit(solution)/shard_map/ppermute | solution.py:302
  65.0 3.2 %collective-permute-done.8 = bf16[2,144,192]{2,1,0:T(8,128)(2,1)S(1)} collective-permute-done((bf16[2,144,192]{2,1,0:T(8,128)(2,1)S(1)}, bf16[2,144,192]{2,1,0:T(8,128)(2,1)S(1)}, u32[]{:S(2)}, u32[]{:S(2)}) %collective-permute-start.8) | collective-permute-done | bytes 110624 | tf_op jit(solution)/shard_map/ppermute | solution.py:312
  69.1 5.8 %all-to-all-start.1 = ((bf16[64,32,128]{2,1,0:T(8,128)(2,1)}), bf16[64,32,128]{2,1,0:T(8,128)(2,1)S(1)}, u32[]{:S(2)}, u32[]{:S(2)}) async-start(bf16[64,32,128]{2,1,0:T(8,128)(2,1)} %broadcast_in_dim.7), calls=%async_computation.1 | async-start | bytes 1048576 | tf_op jit(solution)/shard_map/all_to_all | solution.py:384
  75.3 1.1 %slice_bitcast_fusion = (bf16[8,12,12,192]{3,0,2,1:T(8,128)(2,1)}, bf16[8,12,12,192]{3,0,2,1:T(8,128)(2,1)}) fusion(bf16[2,8,12,12,192]{4,1,3,2,0:T(8,128)(2,1)S(1)} %maximum_bitcast_fusion), kind=kLoop, calls=%fused_computation.2 | loop fusion | bytes 1769472 | tf_op jit(solution)/shard_map/squeeze | solution.py:403
  76.4 16.9 %all-to-all-done.1 = bf16[64,32,128]{2,1,0:T(8,128)(2,1)S(1)} async-done(((bf16[64,32,128]{2,1,0:T(8,128)(2,1)}), bf16[64,32,128]{2,1,0:T(8,128)(2,1)S(1)}, u32[]{:S(2)}, u32[]{:S(2)}) %all-to-all-start.1) | async-done | bytes 524320 | tf_op jit(solution)/shard_map/all_to_all | solution.py:384
  93.3 1.3 %collective-permute-start.10 = (bf16[64,9,128]{2,1,0:T(8,128)(2,1)S(1)}, bf16[64,9,128]{2,1,0:T(8,128)(2,1)S(1)}, u32[]{:S(2)}, u32[]{:S(2)}) collective-permute-start(bf16[64,9,128]{2,1,0:T(8,128)(2,1)S(1)} %slice.76), channel_id=1, source_target_pairs={{0,1},{1,0},{2,3},{3,2},{4,5},{5,4},{6,7},{7,6},{8,9},{9,8},{10,11... | collective-permute-start | bytes 442376 | tf_op jit(solution)/shard_map/ppermute | solution.py:302
  (63 shorter events, 8.0 us)
Async XLA Ops:
  0.6 16.0 %copy-start.1 = (f32[2,4,6,3312]{3,1,2,0:T(4,128)S(1)}, f32[2,4,6,3312]{3,1,2,0:T(4,128)}, u32[]{:S(2)}) copy-start(f32[2,4,6,3312]{3,1,2,0:T(4,128)} %param.18) | copy-start | bytes 1907716
  2.9 18.4 %collective-permute-start.3 = (bf16[2,288,192]{2,1,0:T(8,128)(2,1)}, bf16[2,288,192]{2,1,0:T(8,128)(2,1)S(1)}, u32[]{:S(2)}, u32[]{:S(2)}) collective-permute-start(bf16[2,288,192]{2,1,0:T(8,128)(2,1)} %bitcast.75), channel_id=1, source_target_pairs={{0,4},{1,5},{2,6},{3,7},{4,8},{5,9},{6,10},{7,11},{8,12},{9,13},{1... | collective-permute-start | bytes 663560 | tf_op jit(solution)/shard_map/ppermute | solution.py:312
  5.5 22.3 %collective-permute-start = (bf16[2,144,192]{2,1,0:T(8,128)(2,1)}, bf16[2,144,192]{2,1,0:T(8,128)(2,1)S(1)}, u32[]{:S(2)}, u32[]{:S(2)}) collective-permute-start(bf16[2,144,192]{2,1,0:T(8,128)(2,1)} %bitcast.78), channel_id=1, source_target_pairs={{0,1},{1,2},{2,3},{3,0},{4,5},{5,6},{6,7},{7,4},{8,9},{9,10},{10,1... | collective-permute-start | bytes 331784 | tf_op jit(solution)/shard_map/ppermute | solution.py:312
  9.0 18.7 %collective-permute-start.1 = (bf16[2,144,192]{2,1,0:T(8,128)(2,1)}, bf16[2,144,192]{2,1,0:T(8,128)(2,1)S(1)}, u32[]{:S(2)}, u32[]{:S(2)}) collective-permute-start(bf16[2,144,192]{2,1,0:T(8,128)(2,1)} %bitcast.77), channel_id=1, source_target_pairs={{0,253},{1,254},{2,255},{3,252},{4,1},{5,2},{6,3},{7,0},{8,5},{9,6... | collective-permute-start | bytes 331784 | tf_op jit(solution)/shard_map/ppermute | solution.py:312
  14.8 13.0 %collective-permute-start.2 = (bf16[2,144,192]{2,1,0:T(8,128)(2,1)}, bf16[2,144,192]{2,1,0:T(8,128)(2,1)S(1)}, u32[]{:S(2)}, u32[]{:S(2)}) collective-permute-start(bf16[2,144,192]{2,1,0:T(8,128)(2,1)} %bitcast.76), channel_id=1, source_target_pairs={{0,252},{1,253},{2,254},{3,255},{4,0},{5,1},{6,2},{7,3},{8,4},{9,5... | collective-permute-start | bytes 331784 | tf_op jit(solution)/shard_map/ppermute | solution.py:312
  16.7 1.4 %copy-start = (bf16[828,896]{1,0:T(8,128)(2,1)S(1)}, bf16[828,896]{1,0:T(8,128)(2,1)}, u32[]{:S(2)}) copy-start(bf16[828,896]{1,0:T(8,128)(2,1)} %constant.34.clone.hot_ref) | copy-start | bytes 4451332
  18.0 3.3 %copy-start.2 = (bf16[2,6,6,8,192]{4,3,2,1,0:T(8,128)(2,1)S(1)}, bf16[2,6,6,8,192]{4,3,2,1,0:T(8,128)(2,1)}, u32[]{:S(2)}) copy-start(bf16[2,6,6,8,192]{4,3,2,1,0:T(8,128)(2,1)} %get-tuple-element.34) | copy-start | bytes 663556
  18.0 3.3 %copy-start.3 = (bf16[192,576]{1,0:T(8,128)(2,1)S(1)}, bf16[192,576]{1,0:T(8,128)(2,1)}, u32[]{:S(2)}) copy-start(bf16[192,576]{1,0:T(8,128)(2,1)} %refs_8_.1) | copy-start | bytes 663556
  18.0 3.3 %copy-start.5 = (bf16[192,192]{1,0:T(8,128)(2,1)S(1)}, bf16[192,192]{1,0:T(8,128)(2,1)}, u32[]{:S(2)}) copy-start(bf16[192,192]{1,0:T(8,128)(2,1)} %refs_9_.1) | copy-start | bytes 221188
  18.0 3.3 %copy-start.6 = (f32[192]{0:T(256)S(1)}, f32[192]{0:T(256)}, u32[]{:S(2)}) copy-start(f32[192]{0:T(256)} %param.14) | copy-start | bytes 2308
  18.0 3.3 %copy-start.7 = (f32[192]{0:T(256)S(1)}, f32[192]{0:T(256)}, u32[]{:S(2)}) copy-start(f32[192]{0:T(256)} %param.15) | copy-start | bytes 2308
  18.1 3.3 %copy-start.8 = (bf16[576,576]{1,0:T(8,128)(2,1)S(1)}, bf16[576,576]{1,0:T(8,128)(2,1)}, u32[]{:S(2)}) copy-start(bf16[576,576]{1,0:T(8,128)(2,1)} %constant.35.clone.refs_2_.refs_4_) | copy-start | bytes 1990660
  18.1 3.3 %copy-start.9 = (bf16[576,576]{1,0:T(8,128)(2,1)S(1)}, bf16[576,576]{1,0:T(8,128)(2,1)}, u32[]{:S(2)}) copy-start(bf16[576,576]{1,0:T(8,128)(2,1)} %constant.36.clone.refs_3_.refs_5_) | copy-start | bytes 1990660
  21.4 6.4 %copy-start.4 = (bf16[2,3,6,8,192]{4,3,2,1,0:T(8,128)(2,1)S(1)}, bf16[2,3,6,8,192]{4,3,2,1,0:T(8,128)(2,1)}, u32[]{:S(2)}) copy-start(bf16[2,3,6,8,192]{4,3,2,1,0:T(8,128)(2,1)} %get-tuple-element.31) | copy-start | bytes 331780
  34.7 2.5 %collective-permute-start.4 = (bf16[64,11,128]{2,1,0:T(8,128)(2,1)S(1)}, bf16[64,11,128]{2,1,0:T(8,128)(2,1)S(1)}, u32[]{:S(2)}, u32[]{:S(2)}) collective-permute-start(bf16[64,11,128]{2,1,0:T(8,128)(2,1)S(1)} %dynamic-slice_bitcast_fusion), channel_id=1, source_target_pairs={{0,1},{1,0},{2,3},{3,2},{4,5},{5,4},{6,7},{7,6},{8,9},{9,8},{10,11... | collective-permute-start | bytes 540680 | tf_op jit(solution)/shard_map/ppermute | solution.py:302
  38.3 22.1 %all-to-all-start = ((bf16[64,32,128]{2,1,0:T(8,128)(2,1)}), bf16[64,32,128]{2,1,0:T(8,128)(2,1)S(1)}, u32[]{:S(2)}, u32[]{:S(2)}) async-start(bf16[64,32,128]{2,1,0:T(8,128)(2,1)} %pad_maximum_fusion), calls=%async_computation | async-start | bytes 1048576 | tf_op jit(solution)/shard_map/all_to_all | solution.py:375
  43.1 21.9 %collective-permute-start.7 = (bf16[2,144,192]{2,1,0:T(8,128)(2,1)S(1)}, bf16[2,144,192]{2,1,0:T(8,128)(2,1)S(1)}, u32[]{:S(2)}, u32[]{:S(2)}) collective-permute-start(bf16[2,144,192]{2,1,0:T(8,128)(2,1)S(1)} %get-tuple-element.41), channel_id=1, source_target_pairs={{0,4},{1,5},{2,6},{3,7},{4,8},{5,9},{6,10},{7,11},{8,12},{9,13},{1... | collective-permute-start | bytes 331784 | tf_op jit(solution)/shard_map/ppermute | solution.py:312
  44.2 24.1 %collective-permute-start.8 = (bf16[2,144,192]{2,1,0:T(8,128)(2,1)S(1)}, bf16[2,144,192]{2,1,0:T(8,128)(2,1)S(1)}, u32[]{:S(2)}, u32[]{:S(2)}) collective-permute-start(bf16[2,144,192]{2,1,0:T(8,128)(2,1)S(1)} %get-tuple-element.42), channel_id=1, source_target_pairs={{0,7},{1,4},{2,5},{3,6},{4,11},{5,8},{6,9},{7,10},{8,15},{9,12},{1... | collective-permute-start | bytes 331784 | tf_op jit(solution)/shard_map/ppermute | solution.py:312
  46.4 21.8 %collective-permute-start.9 = (bf16[2,144,192]{2,1,0:T(8,128)(2,1)S(1)}, bf16[2,144,192]{2,1,0:T(8,128)(2,1)S(1)}, u32[]{:S(2)}, u32[]{:S(2)}) collective-permute-start(bf16[2,144,192]{2,1,0:T(8,128)(2,1)S(1)} %get-tuple-element.43), channel_id=1, source_target_pairs={{0,3},{1,0},{2,1},{3,2},{4,7},{5,4},{6,5},{7,6},{8,11},{9,8},{10,9... | collective-permute-start | bytes 331784 | tf_op jit(solution)/shard_map/ppermute | solution.py:312
  47.9 20.3 %collective-permute-start.6 = (bf16[2,288,192]{2,1,0:T(8,128)(2,1)S(1)}, bf16[2,288,192]{2,1,0:T(8,128)(2,1)S(1)}, u32[]{:S(2)}, u32[]{:S(2)}) collective-permute-start(bf16[2,288,192]{2,1,0:T(8,128)(2,1)S(1)} %get-tuple-element.40), channel_id=1, source_target_pairs={{0,252},{1,253},{2,254},{3,255},{4,0},{5,1},{6,2},{7,3},{8,4},{9,5... | collective-permute-start | bytes 663560 | tf_op jit(solution)/shard_map/ppermute | solution.py:312
  60.5 4.5 %collective-permute-start.5 = (f32[11,128]{1,0:T(8,128)S(1)}, f32[11,128]{1,0:T(8,128)S(1)}, u32[]{:S(2)}, u32[]{:S(2)}) collective-permute-start(f32[11,128]{1,0:T(8,128)S(1)} %slice.73), channel_id=1, source_target_pairs={{0,2},{2,0},{1,3},{3,1},{4,6},{6,4},{5,7},{7,5},{8,10},{10,8},{9,1... | collective-permute-start | bytes 16904 | tf_op jit(solution)/shard_map/ppermute | solution.py:302
  69.1 24.2 %all-to-all-start.1 = ((bf16[64,32,128]{2,1,0:T(8,128)(2,1)}), bf16[64,32,128]{2,1,0:T(8,128)(2,1)S(1)}, u32[]{:S(2)}, u32[]{:S(2)}) async-start(bf16[64,32,128]{2,1,0:T(8,128)(2,1)} %broadcast_in_dim.7), calls=%async_computation.1 | async-start | bytes 1048576 | tf_op jit(solution)/shard_map/all_to_all | solution.py:384
  74.9 19.7 %collective-permute-start.11 = (f32[2,128]{1,0:T(2,128)S(1)}, f32[2,128]{1,0:T(2,128)S(1)}, u32[]{:S(2)}, u32[]{:S(2)}) collective-permute-start(f32[2,128]{1,0:T(2,128)S(1)} %slice.79), channel_id=1, source_target_pairs={{0,1},{1,0},{2,3},{3,2},{4,5},{5,4},{6,7},{7,6},{8,9},{9,8},{10,11... | collective-permute-start | bytes 3080 | tf_op jit(solution)/shard_map/ppermute | solution.py:302
  93.3 3.4 %collective-permute-start.10 = (bf16[64,9,128]{2,1,0:T(8,128)(2,1)S(1)}, bf16[64,9,128]{2,1,0:T(8,128)(2,1)S(1)}, u32[]{:S(2)}, u32[]{:S(2)}) collective-permute-start(bf16[64,9,128]{2,1,0:T(8,128)(2,1)S(1)} %slice.76), channel_id=1, source_target_pairs={{0,1},{1,0},{2,3},{3,2},{4,5},{5,4},{6,7},{7,6},{8,9},{9,8},{10,11... | collective-permute-start | bytes 442376 | tf_op jit(solution)/shard_map/ppermute | solution.py:302

commit v3 on v2

--- a/solution.py
+++ b/solution.py
@@ -381,7 +381,9 @@
     shard = jnp.concatenate((bsum, wsum), axis=0).astype(BF16)
     shard = jnp.pad(shard, ((0, 1), (0, 0)))
     shard, left, bottom, corner, above = lax.optimization_barrier((shard, left, bottom, corner, above))
-    spread = lax.all_to_all(jnp.broadcast_to(shard, (64,) + shard.shape), LON, 0, 0, tiled=True)
+    column = lax.all_to_all(jnp.broadcast_to(shard, (8,) + shard.shape), "z", 0, 0, tiled=True)
+    spread = lax.all_to_all(jnp.broadcast_to(column, (8,) + column.shape), ("xl", "y"), 0, 0, tiled=True)
+    spread = spread.reshape((64,) + shard.shape)
     bias_grad = spread[:, :20].reshape(64, 2560)[:, :2484].reshape(2, ZWIN, HEADS, POSITIONS)
     whalf = spread[:, 20:29]
     nhalf = wsum[9:11]

time: 99 us -> 98 us (0.990)
  waiting for transfers between devices: 32.3 us -> 19.2 us
  blocking collectives: 0 us -> 9.6 us
  starting transfers between devices: 37.4 us -> 39.8 us
    all_to_all x1, waiting for transfers between devices: 16.9 us -> 3.83 us  [on_device(): lax.all_to_all(jnp.broadcast_to(column, (8,) + column.shape), ('xl', 'y')...]
    all_to_all x0 -> x1, blocking collectives: none -> 9.6 us  [on_device(): lax.all_to_all(jnp.broadcast_to(shard, (8,) + shard.shape), 'z', 0, 0, ti...]
    ppermute x4, starting transfers between devices: 5.26 us -> 9.44 us  [along(): lax.ppermute(block, axis, [(i, (i + distance) % size) for i in range(size)])]
    all_to_all x1, starting transfers between devices: 5.78 us -> 3.96 us  [on_device(): lax.all_to_all(jnp.broadcast_to(column, (8,) + column.shape), ('xl', 'y')...]
where the time goes in v3:
time: 98 us; the launch traced here: 97.6 us
  starting transfers between devices  39.8 us (41%)
  waiting for transfers between devices  19.2 us (20%)
  Pallas kernels  18.2 us (19%)
  blocking collectives  9.6 us (10%)
  local copies, waits for them, and re-layouts  7.61 us (8%)
  other arithmetic  2.29 us (2%)
    ppermute x8, starting transfers between devices, across(): return lax.ppermute(block, LON + LAT, route)  21.6 us
    pallas_call x2, Pallas kernels, attend(): pl.pallas_call(functools.partial(kernel, first), grid=(1,), in_specs=own...  13.2 us
    all_to_all x1, blocking collectives, on_device(): lax.all_to_all(jnp.broadcast_to(shard, (8,) + shard.shape), 'z', 0, 0, ti...  9.6 us
    ppermute x4, starting transfers between devices, along(): lax.ppermute(block, axis, [(i, (i + distance) % size) for i in range(size)])  9.44 us
    all_to_all x1, waiting for transfers between devices, on_device(): parts = lax.all_to_all(payload, LON, 0, 0, tiled=True)  9.41 us
    all_to_all x1, starting transfers between devices, on_device(): parts = lax.all_to_all(payload, LON, 0, 0, tiled=True)  4.79 us
    all_to_all x1, starting transfers between devices, on_device(): lax.all_to_all(jnp.broadcast_to(column, (8,) + column.shape), ('xl', 'y')...  3.96 us
    all_to_all x1, waiting for transfers between devices, on_device(): lax.all_to_all(jnp.broadcast_to(column, (8,) + column.shape), ('xl', 'y')...  3.83 us
  transfers between devices with their start and end apart: 14, of which 6 were waited for; matrix products, arithmetic and copies ran while one was open for 5% of the time, Pallas kernels for 9%

profile of v3, /device:TPU:1, one launch (start us, length us, event | category | flops | bytes accessed | tf_op | source)
XLA Modules:
  0.0 97.6 jit_solution(3517901034953671086)
XLA Ops:
  0.6 2.3 %pack.1 = (bf16[2,6,6,8,192]{4,3,2,1,0:T(8,128)(2,1)}, bf16[2,3,6,8,192]{4,3,2,1,0:T(8,128)(2,1)}, bf16[2,3,6,8,192]{4,3,2,1,0:T(8,128)(2,1)}, bf16[2,3,6,8,192]...) custom-call(bf16[12,12,8,192]{3,2,1,0:T(8,128)(2,1)} %bitcast.69, ...), custom_call_target="tpu_custom_call" | custom-call | tf_op jit(solution)/shard_map/pack/pallas_call | solution.py:334
  2.9 2.5 %collective-permute-start.3 = (bf16[2,288,192]{2,1,0:T(8,128)(2,1)}, bf16[2,288,192]{2,1,0:T(8,128)(2,1)S(1)}, u32[]{:S(2)}, u32[]{:S(2)}) collective-permute-start(bf16[2,288,192]{2,1,0:T(8,128)(2,1)} %bitcast.79), channel_id=1, source_target_pairs={{0,4},{1,5},{2,6},{3,7},{4,8},{5,9},{6,10},{7,11},{8,12},{9,13},{1... | collective-permute-start | bytes 663560 | tf_op jit(solution)/shard_map/ppermute | solution.py:312
  5.5 3.6 %collective-permute-start = (bf16[2,144,192]{2,1,0:T(8,128)(2,1)}, bf16[2,144,192]{2,1,0:T(8,128)(2,1)S(1)}, u32[]{:S(2)}, u32[]{:S(2)}) collective-permute-start(bf16[2,144,192]{2,1,0:T(8,128)(2,1)} %bitcast.82), channel_id=1, source_target_pairs={{0,1},{1,2},{2,3},{3,0},{4,5},{5,6},{6,7},{7,4},{8,9},{9,10},{10,1... | collective-permute-start | bytes 331784 | tf_op jit(solution)/shard_map/ppermute | solution.py:312
  9.0 5.7 %collective-permute-start.1 = (bf16[2,144,192]{2,1,0:T(8,128)(2,1)}, bf16[2,144,192]{2,1,0:T(8,128)(2,1)S(1)}, u32[]{:S(2)}, u32[]{:S(2)}) collective-permute-start(bf16[2,144,192]{2,1,0:T(8,128)(2,1)} %bitcast.81), channel_id=1, source_target_pairs={{0,253},{1,254},{2,255},{3,252},{4,1},{5,2},{6,3},{7,0},{8,5},{9,6... | collective-permute-start | bytes 331784 | tf_op jit(solution)/shard_map/ppermute | solution.py:312
  14.8 1.9 %collective-permute-start.2 = (bf16[2,144,192]{2,1,0:T(8,128)(2,1)}, bf16[2,144,192]{2,1,0:T(8,128)(2,1)S(1)}, u32[]{:S(2)}, u32[]{:S(2)}) collective-permute-start(bf16[2,144,192]{2,1,0:T(8,128)(2,1)} %bitcast.80), channel_id=1, source_target_pairs={{0,252},{1,253},{2,254},{3,255},{4,0},{5,1},{6,2},{7,3},{8,4},{9,5... | collective-permute-start | bytes 331784 | tf_op jit(solution)/shard_map/ppermute | solution.py:312
  16.7 1.4 %copy-done = bf16[828,896]{1,0:T(8,128)(2,1)S(1)} copy-done((bf16[828,896]{1,0:T(8,128)(2,1)S(1)}, bf16[828,896]{1,0:T(8,128)(2,1)}, u32[]{:S(2)}) %copy-start) | copy-done | bytes 1483800
  18.1 2.8 %table.1 = f32[4608,128]{1,0:T(8,128)S(1)} custom-call(s32[1]{0:T(128)} %bitcast.8.lat_ref, f32[2,6,4,3312]{3,2,1,0:T(4,128)S(1)} %bitcast.52, bf16[828,896]{1,0:T(8,128)(2,1)S(1)} %copy-done), custom_call_target="tpu_custom_call" | custom-call | flops 854654976 | bytes 5000000 | tf_op jit(solution)/shard_map/table/pallas_call | solution.py:278
  21.4 6.3 %attend_first.1 = (bf16[2,288,192]{2,1,0:T(8,128)(2,1)S(1)}, bf16[2,288,192]{2,1,0:T(8,128)(2,1)S(1)}, f32[1,4,192,128]{3,2,1,0:T(8,128)S(1)}, f32[1152,128]{1,0:T(8,128)S(1)}, f32[8,192]{1,0:T(8,128)S(1)}) custom-call(bf16[2,288,192]{2,1,0:T(8,128)(2,1)S(1)} %collective-permute-done.3.refs_0_, bf16[2,288,192]{2,1,0:T(8,128)(2,1)S(1)} %bitcast.55, ...), custom_call_target="tpu_custom_call" | custom-call | flops 3000000000 | bytes 4000000 | tf_op jit(solution)/shard_map/attend_first/pallas_call | solution.py:223
  27.8 6.9 %attend_last.1 = (bf16[2,144,192]{2,1,0:T(8,128)(2,1)S(1)}, bf16[2,144,192]{2,1,0:T(8,128)(2,1)S(1)}, bf16[2,144,192]{2,1,0:T(8,128)(2,1)S(1)}, bf16[2,144,192]{...) custom-call(bf16[2,144,192]{2,1,0:T(8,128)(2,1)S(1)} %collective-permute-done.refs_0_, ...), custom_call_target="tpu_custom_call" | custom-call | flops 3000000000 | bytes 4000000 | tf_op jit(solution)/shard_map/attend_last/pallas_call | solution.py:223
  34.7 1.4 %collective-permute-start.4 = (bf16[64,11,128]{2,1,0:T(8,128)(2,1)S(1)}, bf16[64,11,128]{2,1,0:T(8,128)(2,1)S(1)}, u32[]{:S(2)}, u32[]{:S(2)}) collective-permute-start(bf16[64,11,128]{2,1,0:T(8,128)(2,1)S(1)} %dynamic-slice_bitcast_fusion), channel_id=1, source_target_pairs={{0,1},{1,0},{2,3},{3,2},{4,5},{5,4},{6,7},{7,6},{8,9},{9,8},{10,11... | collective-permute-start | bytes 540680 | tf_op jit(solution)/shard_map/ppermute | solution.py:302
  38.3 4.8 %all-to-all-start = ((bf16[64,32,128]{2,1,0:T(8,128)(2,1)}), bf16[64,32,128]{2,1,0:T(8,128)(2,1)S(1)}, u32[]{:S(2)}, u32[]{:S(2)}) async-start(bf16[64,32,128]{2,1,0:T(8,128)(2,1)} %pad_maximum_fusion), calls=%async_computation | async-start | bytes 1048576 | tf_op jit(solution)/shard_map/all_to_all | solution.py:375
  43.1 1.1 %collective-permute-start.7 = (bf16[2,144,192]{2,1,0:T(8,128)(2,1)S(1)}, bf16[2,144,192]{2,1,0:T(8,128)(2,1)S(1)}, u32[]{:S(2)}, u32[]{:S(2)}) collective-permute-start(bf16[2,144,192]{2,1,0:T(8,128)(2,1)S(1)} %get-tuple-element.41), channel_id=1, source_target_pairs={{0,4},{1,5},{2,6},{3,7},{4,8},{5,9},{6,10},{7,11},{8,12},{9,13},{1... | collective-permute-start | bytes 331784 | tf_op jit(solution)/shard_map/ppermute | solution.py:312
  44.2 2.3 %collective-permute-start.8 = (bf16[2,144,192]{2,1,0:T(8,128)(2,1)S(1)}, bf16[2,144,192]{2,1,0:T(8,128)(2,1)S(1)}, u32[]{:S(2)}, u32[]{:S(2)}) collective-permute-start(bf16[2,144,192]{2,1,0:T(8,128)(2,1)S(1)} %get-tuple-element.42), channel_id=1, source_target_pairs={{0,7},{1,4},{2,5},{3,6},{4,11},{5,8},{6,9},{7,10},{8,15},{9,12},{1... | collective-permute-start | bytes 331784 | tf_op jit(solution)/shard_map/ppermute | solution.py:312
  46.4 1.5 %collective-permute-start.9 = (bf16[2,144,192]{2,1,0:T(8,128)(2,1)S(1)}, bf16[2,144,192]{2,1,0:T(8,128)(2,1)S(1)}, u32[]{:S(2)}, u32[]{:S(2)}) collective-permute-start(bf16[2,144,192]{2,1,0:T(8,128)(2,1)S(1)} %get-tuple-element.43), channel_id=1, source_target_pairs={{0,3},{1,0},{2,1},{3,2},{4,7},{5,4},{6,5},{7,6},{8,11},{9,8},{10,9... | collective-permute-start | bytes 331784 | tf_op jit(solution)/shard_map/ppermute | solution.py:312
  47.9 3.0 %collective-permute-start.6 = (bf16[2,288,192]{2,1,0:T(8,128)(2,1)S(1)}, bf16[2,288,192]{2,1,0:T(8,128)(2,1)S(1)}, u32[]{:S(2)}, u32[]{:S(2)}) collective-permute-start(bf16[2,288,192]{2,1,0:T(8,128)(2,1)S(1)} %get-tuple-element.40), channel_id=1, source_target_pairs={{0,252},{1,253},{2,254},{3,255},{4,0},{5,1},{6,2},{7,3},{8,4},{9,5... | collective-permute-start | bytes 663560 | tf_op jit(solution)/shard_map/ppermute | solution.py:312
  50.9 9.4 %all-to-all-done = bf16[64,32,128]{2,1,0:T(8,128)(2,1)S(1)} async-done(((bf16[64,32,128]{2,1,0:T(8,128)(2,1)}), bf16[64,32,128]{2,1,0:T(8,128)(2,1)S(1)}, u32[]{:S(2)}, u32[]{:S(2)}) %all-to-all-start) | async-done | bytes 524320 | tf_op jit(solution)/shard_map/all_to_all | solution.py:375
  60.5 2.5 %collective-permute-start.5 = (f32[11,128]{1,0:T(8,128)S(1)}, f32[11,128]{1,0:T(8,128)S(1)}, u32[]{:S(2)}, u32[]{:S(2)}) collective-permute-start(f32[11,128]{1,0:T(8,128)S(1)} %slice.73), channel_id=1, source_target_pairs={{0,2},{2,0},{1,3},{3,1},{4,6},{6,4},{5,7},{7,5},{8,10},{10,8},{9,1... | collective-permute-start | bytes 16904 | tf_op jit(solution)/shard_map/ppermute | solution.py:302
  63.8 1.2 %collective-permute-done.5 = f32[11,128]{1,0:T(8,128)S(1)} collective-permute-done((f32[11,128]{1,0:T(8,128)S(1)}, f32[11,128]{1,0:T(8,128)S(1)}, u32[]{:S(2)}, u32[]{:S(2)}) %collective-permute-start.5) | collective-permute-done | bytes 5664 | tf_op jit(solution)/shard_map/ppermute | solution.py:302
  65.0 3.2 %collective-permute-done.8 = bf16[2,144,192]{2,1,0:T(8,128)(2,1)S(1)} collective-permute-done((bf16[2,144,192]{2,1,0:T(8,128)(2,1)S(1)}, bf16[2,144,192]{2,1,0:T(8,128)(2,1)S(1)}, u32[]{:S(2)}, u32[]{:S(2)}) %collective-permute-start.8) | collective-permute-done | bytes 110624 | tf_op jit(solution)/shard_map/ppermute | solution.py:312
  68.2 9.6 %all_to_all.15 = bf16[8,32,128]{2,1,0:T(8,128)(2,1)S(1)} all-to-all(bf16[8,32,128]{2,1,0:T(8,128)(2,1)S(1)} %broadcast_in_dim.10), channel_id=1, replica_groups=mesh['xl'=2,'y'=4,'z'=8,'xh'=2,'c'=2] {'z'}, dimensions={0} | all-to-all | bytes 131072 | tf_op jit(solution)/shard_map/all_to_all | solution.py:384
  78.7 4.0 %all-to-all-start.2 = ((bf16[8,8,32,128]{3,2,1,0:T(8,128)(2,1)}), bf16[8,8,32,128]{3,2,1,0:T(8,128)(2,1)S(1)}, u32[]{:S(2)}, u32[]{:S(2)}) async-start(bf16[8,8,32,128]{3,2,1,0:T(8,128)(2,1)} %broadcast_in_dim.11), calls=%async_computation.2 | async-start | bytes 1048576 | tf_op jit(solution)/shard_map/all_to_all | solution.py:385
  82.7 2.0 %collective-permute-start.11 = (f32[2,128]{1,0:T(2,128)S(1)}, f32[2,128]{1,0:T(2,128)S(1)}, u32[]{:S(2)}, u32[]{:S(2)}) collective-permute-start(f32[2,128]{1,0:T(2,128)S(1)} %slice.79), channel_id=1, source_target_pairs={{0,1},{1,0},{2,3},{3,2},{4,5},{5,4},{6,7},{7,6},{8,9},{9,8},{10,11... | collective-permute-start | bytes 3080 | tf_op jit(solution)/shard_map/ppermute | solution.py:302
  86.1 3.8 %all-to-all-done.2 = bf16[8,8,32,128]{3,2,1,0:T(8,128)(2,1)S(1)} async-done(((bf16[8,8,32,128]{3,2,1,0:T(8,128)(2,1)}), bf16[8,8,32,128]{3,2,1,0:T(8,128)(2,1)S(1)}, u32[]{:S(2)}, u32[]{:S(2)}) %all-to-all-start.2) | async-done | bytes 524320 | tf_op jit(solution)/shard_map/all_to_all | solution.py:385
  90.0 3.5 %collective-permute-start.10 = (bf16[64,9,128]{2,1,0:T(8,128)(2,1)S(1)}, bf16[64,9,128]{2,1,0:T(8,128)(2,1)S(1)}, u32[]{:S(2)}, u32[]{:S(2)}) collective-permute-start(bf16[64,9,128]{2,1,0:T(8,128)(2,1)S(1)} %slice.76), channel_id=1, source_target_pairs={{0,1},{1,0},{2,3},{3,2},{4,5},{5,4},{6,7},{7,6},{8,9},{9,8},{10,11... | collective-permute-start | bytes 442376 | tf_op jit(solution)/shard_map/ppermute | solution.py:302
  (65 shorter events, 10.1 us)
Async XLA Ops:
  0.6 16.0 %copy-start.1 = (f32[2,4,6,3312]{3,1,2,0:T(4,128)S(1)}, f32[2,4,6,3312]{3,1,2,0:T(4,128)}, u32[]{:S(2)}) copy-start(f32[2,4,6,3312]{3,1,2,0:T(4,128)} %param.18) | copy-start | bytes 1907716
  2.9 18.4 %collective-permute-start.3 = (bf16[2,288,192]{2,1,0:T(8,128)(2,1)}, bf16[2,288,192]{2,1,0:T(8,128)(2,1)S(1)}, u32[]{:S(2)}, u32[]{:S(2)}) collective-permute-start(bf16[2,288,192]{2,1,0:T(8,128)(2,1)} %bitcast.79), channel_id=1, source_target_pairs={{0,4},{1,5},{2,6},{3,7},{4,8},{5,9},{6,10},{7,11},{8,12},{9,13},{1... | collective-permute-start | bytes 663560 | tf_op jit(solution)/shard_map/ppermute | solution.py:312
  5.5 22.3 %collective-permute-start = (bf16[2,144,192]{2,1,0:T(8,128)(2,1)}, bf16[2,144,192]{2,1,0:T(8,128)(2,1)S(1)}, u32[]{:S(2)}, u32[]{:S(2)}) collective-permute-start(bf16[2,144,192]{2,1,0:T(8,128)(2,1)} %bitcast.82), channel_id=1, source_target_pairs={{0,1},{1,2},{2,3},{3,0},{4,5},{5,6},{6,7},{7,4},{8,9},{9,10},{10,1... | collective-permute-start | bytes 331784 | tf_op jit(solution)/shard_map/ppermute | solution.py:312
  9.0 18.7 %collective-permute-start.1 = (bf16[2,144,192]{2,1,0:T(8,128)(2,1)}, bf16[2,144,192]{2,1,0:T(8,128)(2,1)S(1)}, u32[]{:S(2)}, u32[]{:S(2)}) collective-permute-start(bf16[2,144,192]{2,1,0:T(8,128)(2,1)} %bitcast.81), channel_id=1, source_target_pairs={{0,253},{1,254},{2,255},{3,252},{4,1},{5,2},{6,3},{7,0},{8,5},{9,6... | collective-permute-start | bytes 331784 | tf_op jit(solution)/shard_map/ppermute | solution.py:312
  14.8 13.0 %collective-permute-start.2 = (bf16[2,144,192]{2,1,0:T(8,128)(2,1)}, bf16[2,144,192]{2,1,0:T(8,128)(2,1)S(1)}, u32[]{:S(2)}, u32[]{:S(2)}) collective-permute-start(bf16[2,144,192]{2,1,0:T(8,128)(2,1)} %bitcast.80), channel_id=1, source_target_pairs={{0,252},{1,253},{2,254},{3,255},{4,0},{5,1},{6,2},{7,3},{8,4},{9,5... | collective-permute-start | bytes 331784 | tf_op jit(solution)/shard_map/ppermute | solution.py:312
  16.7 1.4 %copy-start = (bf16[828,896]{1,0:T(8,128)(2,1)S(1)}, bf16[828,896]{1,0:T(8,128)(2,1)}, u32[]{:S(2)}) copy-start(bf16[828,896]{1,0:T(8,128)(2,1)} %constant.34.clone.hot_ref) | copy-start | bytes 4451332
  18.0 3.3 %copy-start.2 = (bf16[2,6,6,8,192]{4,3,2,1,0:T(8,128)(2,1)S(1)}, bf16[2,6,6,8,192]{4,3,2,1,0:T(8,128)(2,1)}, u32[]{:S(2)}) copy-start(bf16[2,6,6,8,192]{4,3,2,1,0:T(8,128)(2,1)} %get-tuple-element.34) | copy-start | bytes 663556
  18.0 3.3 %copy-start.3 = (bf16[192,576]{1,0:T(8,128)(2,1)S(1)}, bf16[192,576]{1,0:T(8,128)(2,1)}, u32[]{:S(2)}) copy-start(bf16[192,576]{1,0:T(8,128)(2,1)} %refs_8_.1) | copy-start | bytes 663556
  18.0 3.3 %copy-start.5 = (bf16[192,192]{1,0:T(8,128)(2,1)S(1)}, bf16[192,192]{1,0:T(8,128)(2,1)}, u32[]{:S(2)}) copy-start(bf16[192,192]{1,0:T(8,128)(2,1)} %refs_9_.1) | copy-start | bytes 221188
  18.0 3.3 %copy-start.6 = (f32[192]{0:T(256)S(1)}, f32[192]{0:T(256)}, u32[]{:S(2)}) copy-start(f32[192]{0:T(256)} %param.14) | copy-start | bytes 2308
  18.0 3.3 %copy-start.7 = (f32[192]{0:T(256)S(1)}, f32[192]{0:T(256)}, u32[]{:S(2)}) copy-start(f32[192]{0:T(256)} %param.15) | copy-start | bytes 2308
  18.1 3.3 %copy-start.8 = (bf16[576,576]{1,0:T(8,128)(2,1)S(1)}, bf16[576,576]{1,0:T(8,128)(2,1)}, u32[]{:S(2)}) copy-start(bf16[576,576]{1,0:T(8,128)(2,1)} %constant.35.clone.refs_2_.refs_4_) | copy-start | bytes 1990660
  18.1 3.3 %copy-start.9 = (bf16[576,576]{1,0:T(8,128)(2,1)S(1)}, bf16[576,576]{1,0:T(8,128)(2,1)}, u32[]{:S(2)}) copy-start(bf16[576,576]{1,0:T(8,128)(2,1)} %constant.36.clone.refs_3_.refs_5_) | copy-start | bytes 1990660
  21.4 6.4 %copy-start.4 = (bf16[2,3,6,8,192]{4,3,2,1,0:T(8,128)(2,1)S(1)}, bf16[2,3,6,8,192]{4,3,2,1,0:T(8,128)(2,1)}, u32[]{:S(2)}) copy-start(bf16[2,3,6,8,192]{4,3,2,1,0:T(8,128)(2,1)} %get-tuple-element.31) | copy-start | bytes 331780
  34.7 2.5 %collective-permute-start.4 = (bf16[64,11,128]{2,1,0:T(8,128)(2,1)S(1)}, bf16[64,11,128]{2,1,0:T(8,128)(2,1)S(1)}, u32[]{:S(2)}, u32[]{:S(2)}) collective-permute-start(bf16[64,11,128]{2,1,0:T(8,128)(2,1)S(1)} %dynamic-slice_bitcast_fusion), channel_id=1, source_target_pairs={{0,1},{1,0},{2,3},{3,2},{4,5},{5,4},{6,7},{7,6},{8,9},{9,8},{10,11... | collective-permute-start | bytes 540680 | tf_op jit(solution)/shard_map/ppermute | solution.py:302
  38.3 22.1 %all-to-all-start = ((bf16[64,32,128]{2,1,0:T(8,128)(2,1)}), bf16[64,32,128]{2,1,0:T(8,128)(2,1)S(1)}, u32[]{:S(2)}, u32[]{:S(2)}) async-start(bf16[64,32,128]{2,1,0:T(8,128)(2,1)} %pad_maximum_fusion), calls=%async_computation | async-start | bytes 1048576 | tf_op jit(solution)/shard_map/all_to_all | solution.py:375
  43.1 21.9 %collective-permute-start.7 = (bf16[2,144,192]{2,1,0:T(8,128)(2,1)S(1)}, bf16[2,144,192]{2,1,0:T(8,128)(2,1)S(1)}, u32[]{:S(2)}, u32[]{:S(2)}) collective-permute-start(bf16[2,144,192]{2,1,0:T(8,128)(2,1)S(1)} %get-tuple-element.41), channel_id=1, source_target_pairs={{0,4},{1,5},{2,6},{3,7},{4,8},{5,9},{6,10},{7,11},{8,12},{9,13},{1... | collective-permute-start | bytes 331784 | tf_op jit(solution)/shard_map/ppermute | solution.py:312
  44.2 24.1 %collective-permute-start.8 = (bf16[2,144,192]{2,1,0:T(8,128)(2,1)S(1)}, bf16[2,144,192]{2,1,0:T(8,128)(2,1)S(1)}, u32[]{:S(2)}, u32[]{:S(2)}) collective-permute-start(bf16[2,144,192]{2,1,0:T(8,128)(2,1)S(1)} %get-tuple-element.42), channel_id=1, source_target_pairs={{0,7},{1,4},{2,5},{3,6},{4,11},{5,8},{6,9},{7,10},{8,15},{9,12},{1... | collective-permute-start | bytes 331784 | tf_op jit(solution)/shard_map/ppermute | solution.py:312
  46.4 21.8 %collective-permute-start.9 = (bf16[2,144,192]{2,1,0:T(8,128)(2,1)S(1)}, bf16[2,144,192]{2,1,0:T(8,128)(2,1)S(1)}, u32[]{:S(2)}, u32[]{:S(2)}) collective-permute-start(bf16[2,144,192]{2,1,0:T(8,128)(2,1)S(1)} %get-tuple-element.43), channel_id=1, source_target_pairs={{0,3},{1,0},{2,1},{3,2},{4,7},{5,4},{6,5},{7,6},{8,11},{9,8},{10,9... | collective-permute-start | bytes 331784 | tf_op jit(solution)/shard_map/ppermute | solution.py:312
  47.9 20.3 %collective-permute-start.6 = (bf16[2,288,192]{2,1,0:T(8,128)(2,1)S(1)}, bf16[2,288,192]{2,1,0:T(8,128)(2,1)S(1)}, u32[]{:S(2)}, u32[]{:S(2)}) collective-permute-start(bf16[2,288,192]{2,1,0:T(8,128)(2,1)S(1)} %get-tuple-element.40), channel_id=1, source_target_pairs={{0,252},{1,253},{2,254},{3,255},{4,0},{5,1},{6,2},{7,3},{8,4},{9,5... | collective-permute-start | bytes 663560 | tf_op jit(solution)/shard_map/ppermute | solution.py:312
  60.5 4.5 %collective-permute-start.5 = (f32[11,128]{1,0:T(8,128)S(1)}, f32[11,128]{1,0:T(8,128)S(1)}, u32[]{:S(2)}, u32[]{:S(2)}) collective-permute-start(f32[11,128]{1,0:T(8,128)S(1)} %slice.73), channel_id=1, source_target_pairs={{0,2},{2,0},{1,3},{3,1},{4,6},{6,4},{5,7},{7,5},{8,10},{10,8},{9,1... | collective-permute-start | bytes 16904 | tf_op jit(solution)/shard_map/ppermute | solution.py:302
  78.7 11.1 %all-to-all-start.2 = ((bf16[8,8,32,128]{3,2,1,0:T(8,128)(2,1)}), bf16[8,8,32,128]{3,2,1,0:T(8,128)(2,1)S(1)}, u32[]{:S(2)}, u32[]{:S(2)}) async-start(bf16[8,8,32,128]{3,2,1,0:T(8,128)(2,1)} %broadcast_in_dim.11), calls=%async_computation.2 | async-start | bytes 1048576 | tf_op jit(solution)/shard_map/all_to_all | solution.py:385
  82.7 10.8 %collective-permute-start.11 = (f32[2,128]{1,0:T(2,128)S(1)}, f32[2,128]{1,0:T(2,128)S(1)}, u32[]{:S(2)}, u32[]{:S(2)}) collective-permute-start(f32[2,128]{1,0:T(2,128)S(1)} %slice.79), channel_id=1, source_target_pairs={{0,1},{1,0},{2,3},{3,2},{4,5},{5,4},{6,7},{7,6},{8,9},{9,8},{10,11... | collective-permute-start | bytes 3080 | tf_op jit(solution)/shard_map/ppermute | solution.py:302
  90.0 5.7 %collective-permute-start.10 = (bf16[64,9,128]{2,1,0:T(8,128)(2,1)S(1)}, bf16[64,9,128]{2,1,0:T(8,128)(2,1)S(1)}, u32[]{:S(2)}, u32[]{:S(2)}) collective-permute-start(bf16[64,9,128]{2,1,0:T(8,128)(2,1)S(1)} %slice.76), channel_id=1, source_target_pairs={{0,1},{1,0},{2,3},{3,2},{4,5},{5,4},{6,7},{7,6},{8,9},{9,8},{10,11... | collective-permute-start | bytes 442376 | tf_op jit(solution)/shard_map/ppermute | solution.py:302
